TPU v7x, 32 devices: a whole 2x2x4 slice. The times are simulated.
32 devices in a mesh: dp: 4 (over y, core), seq: 8 (over z, x).
Axes of the slice: x: 2, y: 2, z: 4, core: 2. Of those that a mesh axis runs over, the one named last changes fastest.
Arguments:
- hidden: bfloat16 [4096, 2048], P(('dp', 'seq')), may hold values from -6 to 6
- queries: bfloat16 [4096, 2048], P(('dp', 'seq')), may hold values from -360 to 360
- values: bfloat16 [4096, 512], P(('dp', 'seq')), may hold values from -6 to 6
- row_target: int32 [4096], P(('dp', 'seq')), may hold values from 0 to 1023, as said below
- key_weight: bfloat16 [2048, 512], P(('dp', 'seq')), may hold values from -0.125 to 0.125
- dialogue_lengths: int32 [4, 16], P('dp'), may hold values from 1 to 256, 1024 in all within a row
- teacher_pick: int32 [4096, 128], P(('dp', 'seq')), may hold values from 0 to 65279
- teacher_prob: float32 [4096, 128], P(('dp', 'seq')), may hold values from 0.02 to 1
Outputs:
- attn_out: bfloat16 [4096, 2048], P(('dp', 'seq'))
- token_loss: float32 [4096], P(('dp', 'seq'))
- weight_grad: float32 [2048, 512], P(('dp', 'seq'))
Inputs may be any that keep to these rules, and one draw needn't show every extreme that they name: Within each pack, row_target holds every position 0 to 1023 once. Of the 128 rows of one device, at most 24 have targets in one block of 128 positions (target // 128 names the block), and in every draw some device sends exactly 24 to some block.
All inputs are finite; a program needn't handle non-finite values.
Results may differ from a plain program's by a relative error of at most 0.012.
The roundings to bfloat16 on the way count: a program that leaves them out, or rounds other values in their place, can miss the bound.
Values may be sent and summed in bfloat16 or wider, within the bound.
A program may use at most 64 MiB of HBM per device.

v0:
```python
import jax
import jax.numpy as jnp
from jax import lax
from jax.sharding import PartitionSpec as P

HEAD_DIM = 128
SPAN = 2


negative = -1e30
rope_base = 500000.0


def shifted(shard, axis, by):
    devices = lax.axis_size(axis)
    pairs = [(i, i + by) for i in range(devices) if 0 <= i + by < devices]
    return lax.ppermute(shard, axis, pairs)


def rotate(matrix, positions, direction):
    count = matrix.shape[0]
    split = matrix.reshape(count, -1, HEAD_DIM)
    halfway = HEAD_DIM // 2
    frequency = rope_base ** (-2.0 * jnp.arange(halfway, dtype=jnp.float32) / HEAD_DIM)
    angle = positions.astype(jnp.float32)[:, None] * frequency[None, :]
    cosine = jnp.cos(angle)[:, None, :]
    sine = direction * jnp.sin(angle)[:, None, :]
    first_half = split[..., :halfway]
    second_half = split[..., halfway:]
    joined = jnp.concatenate(
        [first_half * cosine - second_half * sine, second_half * cosine + first_half * sine],
        axis=-1,
    )
    return joined.reshape(count, -1)


def dialogue_starts(lengths, positions):
    ending = jnp.cumsum(lengths)
    picked = jnp.where(ending[None, :] <= positions[:, None], lengths[None, :], 0)
    return jnp.sum(picked, axis=1)


def block_targets(label_index, label_prob, key_start, width):
    within = label_index - key_start
    columns = jnp.arange(width, dtype=jnp.int32)
    matches = within[..., None] == columns[None, None, None, :]
    table = jnp.sum(jnp.where(matches, label_prob[..., None], 0.0), axis=2)
    return jnp.transpose(table, (1, 0, 2))


def project_keys(inputs, key_weight):
    return jnp.dot(
        inputs,
        lax.all_gather(key_weight, ("dp", "seq"), axis=0, tiled=True),
        preferred_element_type=jnp.float32,
    )


def move_rows(first_rows, second_rows, third_rows, row_places):
    return (
        lax.all_to_all(first_rows, "seq", split_axis=0, concat_axis=0, tiled=True),
        lax.all_to_all(second_rows, "seq", split_axis=0, concat_axis=0, tiled=True),
        lax.all_to_all(third_rows, "seq", split_axis=0, concat_axis=0, tiled=True),
        lax.all_to_all(row_places, "seq", split_axis=0, concat_axis=0, tiled=True),
    )


def guarded(compute, operands):
    return compute(*operands)


def local(
    hidden, queries, values, row_target, key_weight, dialogue_lengths, teacher_pick, teacher_prob
):
    local_rows = hidden.shape[0]
    seq_count = lax.axis_size("seq")
    seq_index = lax.axis_index("seq")
    device_count = seq_count * lax.axis_size("dp")
    capacity = local_rows // seq_count + local_rows // (2 * seq_count)
    head_count = queries.shape[1] // HEAD_DIM
    kv_count = values.shape[1] // HEAD_DIM
    group_size = head_count // kv_count
    top_count = teacher_pick.shape[1] // head_count
    scaling = HEAD_DIM ** (-0.5)
    destination = row_target // local_rows
    offset_in = row_target - destination * local_rows
    one_hot = (destination[:, None] == jnp.arange(seq_count, dtype=jnp.int32)[None, :]).astype(
        jnp.int32
    )
    rank_in = jnp.sum((jnp.cumsum(one_hot, axis=0) - one_hot) * one_hot, axis=1)
    slot_of = destination * capacity + rank_in

    def parcel(data, filler):
        holder = jnp.full((seq_count * capacity,) + data.shape[1:], filler, data.dtype)
        return holder.at[slot_of].set(data)

    def settle(data, places):
        holder = jnp.zeros((local_rows,) + data.shape[1:], data.dtype)
        return holder.at[places].set(data, mode="drop")

    positions = seq_index * local_rows + jnp.arange(local_rows, dtype=jnp.int32)
    received = move_rows(
        parcel(hidden, 0), parcel(queries, 0), parcel(values, 0), parcel(offset_in, local_rows)
    )
    hidden_seq = settle(received[0], received[3])
    queries_seq = settle(received[1], received[3])
    values_seq = settle(received[2], received[3])
    keys_seq = rotate(project_keys(hidden_seq, key_weight), positions, 1.0).astype(jnp.bfloat16)
    starts = dialogue_starts(dialogue_lengths[0], positions)
    reach = (positions - starts + 1)[:, None]
    label_index = (starts[:, None] + teacher_pick % reach).reshape(
        local_rows, head_count, top_count
    )
    label_prob = teacher_prob.reshape(local_rows, head_count, top_count)
    target_mass = jnp.sum(label_prob, axis=2).T.reshape(kv_count, group_size, local_rows)
    entropy = jnp.sum(label_prob * jnp.log(label_prob), axis=(1, 2))
    query_heads = queries_seq.reshape(local_rows, kv_count, group_size, HEAD_DIM)
    earliest = jnp.min(starts)
    blocks = [(keys_seq, values_seq)]
    for distance in range(1, SPAN + 1):
        blocks.append(shifted((keys_seq, values_seq), "seq", distance))

    def scores_of(key_block, key_start):
        key_heads = key_block.reshape(local_rows, kv_count, HEAD_DIM)
        score = (
            jnp.einsum("tkgd,wkd->kgtw", query_heads, key_heads, preferred_element_type=jnp.float32)
            * scaling
        )
        key_pos = key_start + jnp.arange(local_rows, dtype=jnp.int32)
        allowed = (key_pos[None, :] >= starts[:, None]) & (key_pos[None, :] <= positions[:, None])
        held = jnp.where(allowed[None, None], score, negative)
        table = block_targets(label_index, label_prob, key_start, local_rows)
        return (score, held, table.reshape(kv_count, group_size, local_rows, local_rows))

    def first_pass(key_block, key_start):
        score, held, table = scores_of(key_block, key_start)
        block_top = jnp.max(held, axis=-1)
        block_total = jnp.sum(jnp.exp(held - block_top[..., None]), axis=-1)
        return (block_top, block_total, jnp.sum(table * score, axis=-1))

    tops, totals, pickings, alive_list = ([], [], [], [])
    for distance, (key_block, value_block) in enumerate(blocks):
        key_start = (seq_index - distance) * local_rows
        alive = earliest < key_start + local_rows
        alive_list.append((alive, key_start))
        block_top, block_total, picking = guarded(first_pass, (key_block, key_start))
        tops.append(block_top)
        totals.append(block_total)
        pickings.append(picking)
    top_all = jnp.max(jnp.stack(tops), axis=0)
    total_all = jnp.sum(jnp.stack(totals) * jnp.exp(jnp.stack(tops) - top_all[None]), axis=0)
    lse = top_all + jnp.log(total_all)
    picked_all = jnp.sum(jnp.stack(pickings), axis=0)
    token_loss = (
        entropy - jnp.sum(picked_all, axis=(0, 1)) + jnp.sum(target_mass * lse, axis=(0, 1))
    ) / head_count

    def second_pass(key_block, value_block, key_start):
        score, held, table = scores_of(key_block, key_start)
        weight = jnp.exp(held - lse[..., None])
        value_heads = value_block.reshape(local_rows, kv_count, HEAD_DIM)
        partial_value = jnp.einsum(
            "kgtw,wkd->tkgd",
            weight.astype(jnp.bfloat16),
            value_heads,
            preferred_element_type=jnp.float32,
        )
        slope = ((weight * target_mass[..., None] - table) / head_count).astype(jnp.bfloat16)
        gradient = (
            jnp.einsum("kgtw,tkgd->wkd", slope, query_heads, preferred_element_type=jnp.float32)
            * scaling
        )
        return (partial_value, gradient.reshape(local_rows, kv_count * HEAD_DIM))

    output_sum = jnp.zeros((local_rows, kv_count, group_size, HEAD_DIM), jnp.float32)
    block_grads = []
    for distance, (key_block, value_block) in enumerate(blocks):
        alive, key_start = alive_list[distance]
        partial_value, gradient = guarded(second_pass, (key_block, value_block, key_start))
        output_sum = output_sum + partial_value
        block_grads.append(gradient)
    attn_out = output_sum.astype(jnp.bfloat16).reshape(local_rows, head_count * HEAD_DIM)
    rotated_grad = block_grads[0]
    for distance in range(1, SPAN + 1):
        rotated_grad = rotated_grad + shifted(
            block_grads[distance].astype(jnp.bfloat16), "seq", -distance
        ).astype(jnp.float32)
    key_grad = rotate(rotated_grad, positions, -1.0).astype(jnp.bfloat16)
    inverse_root = (local_rows * device_count) ** (-0.5)
    weight_grad = lax.psum_scatter(
        jnp.einsum("td,tc->dc", hidden_seq, key_grad, preferred_element_type=jnp.float32)
        * inverse_root,
        ("dp", "seq"),
        scatter_dimension=0,
        tiled=True,
    )
    return (attn_out, token_loss, weight_grad)


def solution(mesh):
    placed = (
        P(("dp", "seq"), None),
        P(("dp", "seq"), None),
        P(("dp", "seq"), None),
        P(("dp", "seq")),
        P(("dp", "seq"), None),
        P("dp", None),
        P(("dp", "seq"), None),
        P(("dp", "seq"), None),
    )
    return jax.shard_map(
        local,
        mesh=mesh,
        in_specs=placed,
        out_specs=(P(("dp", "seq"), None), P(("dp", "seq")), P(("dp", "seq"), None)),
        check_vma=False,
    )
```

profile of v0, /device:TPU:0, one launch (start us, length us, event | category | flops | bytes accessed | tf_op | source)
XLA Modules:
  0.0 274.0 jit_solution(607761643162922631)
XLA Ops:
  10.0 7.3 %all-to-all-start = ((s32[8,24,1]{1,2,0:T(1,128)}), s32[8,24,1]{1,2,0:T(1,128)S(1)}, u32[]{:S(2)}, u32[]{:S(2)}) async-start(s32[8,24,1]{1,2,0:T(1,128)} %bitcast), calls=%async_computation | async-start | bytes 8192 | tf_op jit(solution)/shard_map/all_to_all | solution.py:64
  17.2 2.8 %scatter_custom_fusion.3 = bf16[192,2048]{1,0:T(8,128)(2,1)} fusion(s32[128]{0:T(128)S(1)} %compare_select_fusion.2, bf16[128,2048]{1,0:T(8,128)(2,1)} %param.8, bf16[]{:T(256)} %constant.25.clone.1), kind=kCustom, calls=%fused_computation.76 | custom fusion | bytes 786944 | tf_op jit(solution)/shard_map/scatter | solution.py:95
  20.0 3.6 %all-to-all-done = s32[8,24,1]{1,2,0:T(1,128)S(1)} async-done(((s32[8,24,1]{1,2,0:T(1,128)}), s32[8,24,1]{1,2,0:T(1,128)S(1)}, u32[]{:S(2)}, u32[]{:S(2)}) %all-to-all-start) | async-done | bytes 800 | tf_op jit(solution)/shard_map/all_to_all | solution.py:64
  23.6 4.2 %all-to-all-start.2 = ((bf16[8,24,2048]{2,1,0:T(8,128)(2,1)}), bf16[8,24,2048]{2,1,0:T(8,128)(2,1)}, u32[]{:S(2)}, u32[]{:S(2)}) async-start(bf16[8,24,2048]{2,1,0:T(8,128)(2,1)} %bitcast.9), calls=%async_computation.2 | async-start | bytes 1572864 | tf_op jit(solution)/shard_map/all_to_all | solution.py:61
  29.5 2.8 %scatter_custom_fusion.5 = bf16[192,2048]{1,0:T(8,128)(2,1)} fusion(s32[128]{0:T(128)S(1)} %compare_select_fusion.2, bf16[128,2048]{1,0:T(8,128)(2,1)} %param.9, bf16[]{:T(256)} %constant.25.clone.1), kind=kCustom, calls=%fused_computation.74 | custom fusion | bytes 786944 | tf_op jit(solution)/shard_map/scatter | solution.py:95
  37.6 9.8 %all-to-all-done.2 = bf16[8,24,2048]{2,1,0:T(8,128)(2,1)} async-done(((bf16[8,24,2048]{2,1,0:T(8,128)(2,1)}), bf16[8,24,2048]{2,1,0:T(8,128)(2,1)}, u32[]{:S(2)}, u32[]{:S(2)}) %all-to-all-start.2) | async-done | bytes 786464 | tf_op jit(solution)/shard_map/all_to_all | solution.py:61
  47.4 4.2 %all-to-all-start.3 = ((bf16[8,24,2048]{2,1,0:T(8,128)(2,1)}), bf16[8,24,2048]{2,1,0:T(8,128)(2,1)}, u32[]{:S(2)}, u32[]{:S(2)}) async-start(bf16[8,24,2048]{2,1,0:T(8,128)(2,1)} %bitcast.151), calls=%async_computation.3 | async-start | bytes 1572864 | tf_op jit(solution)/shard_map/all_to_all | solution.py:62
  51.7 13.2 %select_reduce_fusion.1 = (f32[128,16,128]{2,1,0:T(8,128)}, f32[128,16,128]{2,1,0:T(8,128)}, f32[128,16,128]{2,1,0:T(8,128)}) fusion(s32[128,16,8]{2,1,0:T(8,128)S(1)} %copy.111, f32[128,16,8]{2,1,0:T(8,128)} %copy.109, s32[128,16,8]{2,1,0:T(8,128)S(1)} %copy.113, s32[128,16,8]{2,1,0:T(8,128)S(1)} %copy.107), kind=kLoop, calls=%fused_computation.9 | loop fusion | flops 18087936 | bytes 3407872 | tf_op jit(solution)/shard_map/reduce_sum | solution.py:47
  66.5 2.9 %copy.112 = f32[16,128,128]{1,2,0:T(8,128)} copy(f32[16,128,128]{2,0,1:T(8,128)} %bitcast.149) | data formatting | bytes 2097152 | tf_op jit(solution)/shard_map/transpose | solution.py:48
  72.7 2.4 scatter_custom_fusion.4
  75.2 2.7 scatter_custom_fusion.6
  78.2 14.5 %all-gather.2.cloned.1.call-done = bf16[2048,512]{1,0:T(8,128)(2,1)} async-done(((bf16[64,512]{1,0:T(8,128)(2,1)}), bf16[2048,512]{1,0:T(8,128)(2,1)}) %all-gather.2.cloned.1.call-update) | async-done | bytes 2097168 | tf_op jit(solution)/shard_map/all_gather | solution.py:54
  92.7 2.0 fusion.74
  95.4 3.3 %collective-permute-start = (bf16[128,512]{0,1:T(8,128)(2,1)S(1)}, bf16[128,512]{0,1:T(8,128)(2,1)S(1)}, u32[]{:S(2)}, u32[]{:S(2)}) collective-permute-start(bf16[128,512]{0,1:T(8,128)(2,1)S(1)} %bitcast.179), channel_id=1, source_target_pairs={{0,1},{1,2},{2,3},{3,4},{4,5},{5,6},{6,7},{8,9},{9,10},{10,11},{11... | collective-permute-start | bytes 393224 | tf_op jit(solution)/shard_map/ppermute | solution.py:17
  98.7 2.5 collective-permute-start.1
  102.3 1.8 collective-permute-done.1
  111.1 3.7 %collective-permute-done.4 = bf16[128,512]{0,1:T(8,128)(2,1)S(1)} collective-permute-done((bf16[128,512]{0,1:T(8,128)(2,1)S(1)}, bf16[128,512]{0,1:T(8,128)(2,1)S(1)}, u32[]{:S(2)}, u32[]{:S(2)}) %collective-permute-start.4) | collective-permute-done | bytes 131104 | tf_op jit(solution)/shard_map/ppermute | solution.py:17
  114.8 3.5 %collective-permute-done.5 = bf16[128,512]{0,1:T(8,128)(2,1)S(1)} collective-permute-done((bf16[128,512]{0,1:T(8,128)(2,1)S(1)}, bf16[128,512]{0,1:T(8,128)(2,1)S(1)}, u32[]{:S(2)}, u32[]{:S(2)}) %collective-permute-start.5) | collective-permute-done | bytes 131104 | tf_op jit(solution)/shard_map/ppermute | solution.py:17
  119.0 3.8 %convolution_multiply_fusion = f32[2048,512]{1,0:T(8,128)} fusion(bf16[128,2048]{1,0:T(8,128)(2,1)} %copy-done.6, bf16[128,512]{0,1:T(8,128)(2,1)S(1)} %bitcast.165), kind=kOutput, calls=%fused_computation.13 | convolution fusion | flops 269484032 | bytes 4849664 | tf_op jit(solution)/shard_map/td,tc->dc/dot_general | solution.py:191
  124.3 13.2 %all_to_all.48 = bf16[8,24,512]{2,1,0:T(8,128)(2,1)} all-to-all(bf16[8,24,512]{2,1,0:T(8,128)(2,1)S(1)} %bitcast.154), channel_id=1, replica_groups=mesh['dp'=4,'seq'=8] {'seq'}, dimensions={0} | all-to-all | bytes 393216 | tf_op jit(solution)/shard_map/all_to_all | solution.py:63
  137.5 2.3 scatter_custom_fusion.2
  139.8 3.9 %collective-permute-start.2 = (bf16[128,512]{1,0:T(8,128)(2,1)}, bf16[128,512]{1,0:T(8,128)(2,1)}, u32[]{:S(2)}, u32[]{:S(2)}) collective-permute-start(bf16[128,512]{1,0:T(8,128)(2,1)} %scatter_custom_fusion.2), channel_id=1, source_target_pairs={{0,1},{1,2},{2,3},{3,4},{4,5},{5,6},{6,7},{8,9},{9,10},{10,11},{11... | collective-permute-start | bytes 393224 | tf_op jit(solution)/shard_map/ppermute | solution.py:17
  143.7 2.0 collective-permute-start.3
  153.4 113.8 %reduce-scatter.2.cloned.1.call-done = f32[64,512]{1,0:T(8,128)} async-done(((f32[2048,512]{1,0:T(8,128)}), f32[64,512]{1,0:T(8,128)}) %reduce-scatter.2.cloned.1.call-update) | async-done | bytes 131088 | tf_op jit(solution)/shard_map/reduce_scatter | solution.py:190
  (106 shorter events, 33.1 us)
Async XLA Ops:
  7.2 29.0 %copy-start.9 = (f32[128,128]{1,0:T(8,128)S(1)}, f32[128,128]{1,0:T(8,128)}, u32[]{:S(2)}) copy-start(f32[128,128]{1,0:T(8,128)} %param.15) | copy-start | bytes 196612
  8.3 26.3 %copy-start.13 = (s32[128]{0:T(128)}, s32[128]{0:T(128)S(1)}, u32[]{:S(2)}) copy-start(s32[128]{0:T(128)S(1)} %compare_select_fusion.2) | copy-start | bytes 1540
  10.0 13.6 %all-to-all-start = ((s32[8,24,1]{1,2,0:T(1,128)}), s32[8,24,1]{1,2,0:T(1,128)S(1)}, u32[]{:S(2)}, u32[]{:S(2)}) async-start(s32[8,24,1]{1,2,0:T(1,128)} %bitcast), calls=%async_computation | async-start | bytes 8192 | tf_op jit(solution)/shard_map/all_to_all | solution.py:64
  23.6 23.8 %all-to-all-start.2 = ((bf16[8,24,2048]{2,1,0:T(8,128)(2,1)}), bf16[8,24,2048]{2,1,0:T(8,128)(2,1)}, u32[]{:S(2)}, u32[]{:S(2)}) async-start(bf16[8,24,2048]{2,1,0:T(8,128)(2,1)} %bitcast.9), calls=%async_computation.2 | async-start | bytes 1572864 | tf_op jit(solution)/shard_map/all_to_all | solution.py:61
  27.8 64.8 %all-gather.2.cloned.1.call-start = ((), (), s32[]{:S(2)}) async-start(), calls=%async_computation.5 | async-start | bytes 2162688 | tf_op jit(solution)/shard_map/all_gather | solution.py:54
  47.4 27.8 %all-to-all-start.3 = ((bf16[8,24,2048]{2,1,0:T(8,128)(2,1)}), bf16[8,24,2048]{2,1,0:T(8,128)(2,1)}, u32[]{:S(2)}, u32[]{:S(2)}) async-start(bf16[8,24,2048]{2,1,0:T(8,128)(2,1)} %bitcast.151), calls=%async_computation.3 | async-start | bytes 1572864 | tf_op jit(solution)/shard_map/all_to_all | solution.py:62
  51.6 215.5 %reduce-scatter.2.cloned.1.call-start = ((), (), s32[]{:S(2)}) async-start(), calls=%async_computation.6 | async-start | bytes 4325376 | tf_op jit(solution)/shard_map/reduce_scatter | solution.py:190
  64.9 4.6 %copy-start.7 = (f32[128,16,128]{2,1,0:T(8,128)S(1)}, f32[128,16,128]{2,1,0:T(8,128)}, u32[]{:S(2)}) copy-start(f32[128,16,128]{2,1,0:T(8,128)} %get-tuple-element.18) | copy-start | bytes 3145732
  66.5 35.0 %copy-start.4 = (f32[16,128,128]{1,2,0:T(8,128)}, f32[16,128,128]{1,2,0:T(8,128)S(1)}, u32[]{:S(2)}) copy-start(f32[16,128,128]{1,2,0:T(8,128)S(1)} %copy.110) | copy-start | bytes 3145732
  72.7 22.7 %copy-start.12 = (s32[192,1]{0,1:T(1,128)}, s32[192,1]{0,1:T(1,128)S(1)}, u32[]{:S(2)}) copy-start(s32[192,1]{0,1:T(1,128)S(1)} %compare_select_fusion) | copy-start | bytes 2308
  75.1 26.4 %copy-start.6 = (bf16[128,2048]{1,0:T(8,128)(2,1)}, bf16[128,2048]{1,0:T(8,128)(2,1)S(1)}, u32[]{:S(2)}) copy-start(bf16[128,2048]{1,0:T(8,128)(2,1)S(1)} %scatter_custom_fusion.4) | copy-start | bytes 1572868
  95.4 6.5 %collective-permute-start = (bf16[128,512]{0,1:T(8,128)(2,1)S(1)}, bf16[128,512]{0,1:T(8,128)(2,1)S(1)}, u32[]{:S(2)}, u32[]{:S(2)}) collective-permute-start(bf16[128,512]{0,1:T(8,128)(2,1)S(1)} %bitcast.179), channel_id=1, source_target_pairs={{0,1},{1,2},{2,3},{3,4},{4,5},{5,6},{6,7},{8,9},{9,10},{10,11},{11... | collective-permute-start | bytes 393224 | tf_op jit(solution)/shard_map/ppermute | solution.py:17
  98.7 5.4 %collective-permute-start.1 = (bf16[128,512]{0,1:T(8,128)(2,1)S(1)}, bf16[128,512]{0,1:T(8,128)(2,1)S(1)}, u32[]{:S(2)}, u32[]{:S(2)}) collective-permute-start(bf16[128,512]{0,1:T(8,128)(2,1)S(1)} %bitcast.180), channel_id=1, source_target_pairs={{0,2},{1,3},{2,4},{3,5},{4,6},{5,7},{8,10},{9,11},{10,12},{11,13},... | collective-permute-start | bytes 393224 | tf_op jit(solution)/shard_map/ppermute | solution.py:17
  101.5 9.0 %copy-start = (f32[4,4,128,128]{2,3,1,0:T(8,128)}, f32[4,4,128,128]{2,3,1,0:T(8,128)S(1)}, u32[]{:S(2)}) copy-start(f32[4,4,128,128]{2,3,1,0:T(8,128)S(1)} %get-tuple-element.48) | copy-start | bytes 3145732
  101.6 4.5 %copy-start.3 = (f32[16,128,128]{1,2,0:T(8,128)S(1)}, f32[16,128,128]{1,2,0:T(8,128)}, u32[]{:S(2)}) copy-start(f32[16,128,128]{1,2,0:T(8,128)} %copy.114) | copy-start | bytes 3145732
  101.9 5.1 %copy-start.2 = (f32[16,128,128]{1,2,0:T(8,128)S(1)}, f32[16,128,128]{1,2,0:T(8,128)}, u32[]{:S(2)}) copy-start(f32[16,128,128]{1,2,0:T(8,128)} %copy.112) | copy-start | bytes 3145732
  106.0 4.6 %copy-start.5 = (f32[16,128,128]{1,2,0:T(8,128)S(1)}, f32[16,128,128]{1,2,0:T(8,128)}, u32[]{:S(2)}) copy-start(f32[16,128,128]{1,2,0:T(8,128)} %copy-done.4) | copy-start | bytes 3145732
  108.0 6.9 %collective-permute-start.4 = (bf16[128,512]{0,1:T(8,128)(2,1)S(1)}, bf16[128,512]{0,1:T(8,128)(2,1)S(1)}, u32[]{:S(2)}, u32[]{:S(2)}) collective-permute-start(bf16[128,512]{0,1:T(8,128)(2,1)S(1)} %bitcast.178), channel_id=1, source_target_pairs={{1,0},{2,1},{3,2},{4,3},{5,4},{6,5},{7,6},{9,8},{10,9},{11,10},{12... | collective-permute-start | bytes 393224 | tf_op jit(solution)/shard_map/ppermute | solution.py:17
  109.2 9.0 %collective-permute-start.5 = (bf16[128,512]{0,1:T(8,128)(2,1)S(1)}, bf16[128,512]{0,1:T(8,128)(2,1)S(1)}, u32[]{:S(2)}, u32[]{:S(2)}) collective-permute-start(bf16[128,512]{0,1:T(8,128)(2,1)S(1)} %bitcast.177), channel_id=1, source_target_pairs={{2,0},{3,1},{4,2},{5,3},{6,4},{7,5},{10,8},{11,9},{12,10},{13,11},... | collective-permute-start | bytes 393224 | tf_op jit(solution)/shard_map/ppermute | solution.py:17
  118.9 26.7 %copy-start.10 = (f32[128,128]{1,0:T(8,128)S(1)}, f32[128,128]{1,0:T(8,128)}, u32[]{:S(2)}) copy-start(f32[128,128]{1,0:T(8,128)} %param.15) | copy-start | bytes 196612
  119.0 31.6 %copy-start.1 = (f32[4,4,128,128]{2,3,1,0:T(8,128)S(1)}, f32[4,4,128,128]{2,3,1,0:T(8,128)}, u32[]{:S(2)}) copy-start(f32[4,4,128,128]{2,3,1,0:T(8,128)} %copy-done) | copy-start | bytes 3145732
  139.8 8.1 %collective-permute-start.2 = (bf16[128,512]{1,0:T(8,128)(2,1)}, bf16[128,512]{1,0:T(8,128)(2,1)}, u32[]{:S(2)}, u32[]{:S(2)}) collective-permute-start(bf16[128,512]{1,0:T(8,128)(2,1)} %scatter_custom_fusion.2), channel_id=1, source_target_pairs={{0,1},{1,2},{2,3},{3,4},{4,5},{5,6},{6,7},{8,9},{9,10},{10,11},{11... | collective-permute-start | bytes 393224 | tf_op jit(solution)/shard_map/ppermute | solution.py:17
  143.7 5.2 %collective-permute-start.3 = (bf16[128,512]{1,0:T(8,128)(2,1)}, bf16[128,512]{1,0:T(8,128)(2,1)}, u32[]{:S(2)}, u32[]{:S(2)}) collective-permute-start(bf16[128,512]{1,0:T(8,128)(2,1)} %scatter_custom_fusion.2), channel_id=1, source_target_pairs={{0,2},{1,3},{2,4},{3,5},{4,6},{5,7},{8,10},{9,11},{10,12},{11,13},... | collective-permute-start | bytes 393224 | tf_op jit(solution)/shard_map/ppermute | solution.py:17
  150.5 2.3 copy-start.11
  (1 other events, 0.9 us)
Sparse Core Ops, SparseCore 0:
  31.7 60.9 all-gather.1
  122.9 144.2 reduce-scatter.1
where the time goes:
time: 275 us; the launch traced here: 274 us
  waiting for transfers between devices  152 us (55%)
  local copies, waits for them, and re-layouts  33.4 us (12%)
  starting transfers between devices  30 us (11%)
  other arithmetic  20.9 us (8%)
  between operations  14.6 us (5%)
  blocking collectives  13.2 us (5%)
  matrix products  9.35 us (3%)
    reduce_scatter x1, waiting for transfers between devices, local(): lax.psum_scatter(jnp.einsum('td,tc->dc', hidden_seq, key_grad, preferred_...  114 us
    all_gather x1, waiting for transfers between devices, project_keys(): lax.all_gather(key_weight, ('dp', 'seq'), axis=0, tiled=True)  14.5 us
    ppermute x6, starting transfers between devices, shifted(): return lax.ppermute(shard, axis, pairs)  14.3 us
    all_to_all x1, blocking collectives, move_rows(): lax.all_to_all(third_rows, 'seq', split_axis=0, concat_axis=0, tiled=True)  13.2 us
    reduce_sum x1, other arithmetic, block_targets(): table = jnp.sum(jnp.where(matches, label_prob[..., None], 0.0), axis=2)  13.2 us
    ppermute x6, waiting for transfers between devices, shifted(): return lax.ppermute(shard, axis, pairs)  10.1 us
    all_to_all x1, waiting for transfers between devices, move_rows(): lax.all_to_all(first_rows, 'seq', split_axis=0, concat_axis=0, tiled=True)  9.79 us
    scatter x4, local copies, waits for them, and re-layouts, parcel(): return holder.at[slot_of].set(data)  8.04 us
  transfers between devices with their start and end apart: 11, of which 8 were waited for; matrix products, arithmetic and copies ran while one was open for 18% of the time, Pallas kernels for 0%

commit v1 on v0

v1 whole, which is shorter than its diff:
```python
import functools

import jax
import jax.numpy as jnp
from jax import lax
from jax.experimental import pallas as pl
from jax.experimental.pallas import tpu as pltpu
from jax.sharding import PartitionSpec as P

HEAD_DIM = 128
SPAN = 2
MESH = pl.DeviceIdType.MESH
VMEM_BYTES = 50 * 1024 * 1024

negative = -1e30
rope_base = 500000.0


def angles(positions):
    halfway = HEAD_DIM // 2
    frequency = rope_base ** (-2.0 * jnp.arange(halfway, dtype=jnp.float32) / HEAD_DIM)
    angle = positions.astype(jnp.float32)[:, None] * frequency[None, :]
    cosine = jnp.cos(angle)
    sine = jnp.sin(angle)
    return (
        jnp.concatenate([cosine, cosine], axis=1),
        jnp.concatenate([-sine, sine], axis=1),
    )


def turned(block, cosine, sine):
    return block * cosine + pltpu.roll(block, HEAD_DIM // 2, 1) * sine


def dot(a, b, ca=1, cb=0):
    return lax.dot_general(a, b, (((ca,), (cb,)), ((), ())), preferred_element_type=jnp.float32)


def greet(seq_n, dp_n):
    s = lax.axis_index("seq")
    p = lax.axis_index("dp")
    barrier = pltpu.get_barrier_semaphore()
    for k in range(1, seq_n):
        pl.semaphore_signal(
            barrier, inc=1, device_id=(p, lax.rem(s + k, seq_n)), device_id_type=MESH
        )
    for k in range(1, dp_n):
        pl.semaphore_signal(
            barrier, inc=1, device_id=(lax.rem(p + k, dp_n), s), device_id_type=MESH
        )
    pl.semaphore_wait(barrier, seq_n - 1 + dp_n - 1)


def remote(src, dst, send, recv, p, s):
    return pltpu.make_async_remote_copy(
        src_ref=src, dst_ref=dst, send_sem=send, recv_sem=recv, device_id=(p, s),
        device_id_type=MESH,
    )


def gather_kernel(
    seq_n, dp_n, inside,
    w_ref, hidden_ref, query_ref, value_ref, left_ref, right_ref, spot_ref, cos_ref, sin_ref,
    cols_ref, target_ref,
    q_out, kv_out, cols_out, target_out,
    wall, parcel, got, kparcel, kgot,
    wz_s, wz_r, wx_s, wx_r, wy_s, wy_r, wc_s, wc_r,
    par_s, par_r, col_s, col_r, tgt_s, tgt_r, k_s, k_r, sh_s, sh_r,
):
    s = lax.axis_index("seq")
    p = lax.axis_index("dp")
    rows = query_ref.shape[0]
    qhalf = query_ref.shape[1] // 2
    vhalf = value_ref.shape[1] // 2
    kvn = value_ref.shape[1] // HEAD_DIM
    heads = query_ref.shape[1] // HEAD_DIM
    group = heads // kvn
    slots = got.shape[1]
    cap = slots // 2
    greet(seq_n, dp_n)
    waits = []
    if inside:
        a, b = s // 2, lax.rem(s, 2)
        yb, cc = p // 2, lax.rem(p, 2)
        na, nb = seq_n // 2, dp_n // 2
        wall[p, s] = w_ref[...]
        zc = []
        for k in range(1, na):
            cp = remote(w_ref, wall.at[p, s], wz_s.at[k], wz_r.at[k], p, lax.rem(a + k, na) * 2 + b)
            cp.start()
            zc.append(cp)

    left = left_ref[...]
    right = right_ref[...]
    parcel[:, :, 0:qhalf] = (
        (dot(left, query_ref[:, 0:qhalf]) + dot(right, query_ref[:, qhalf:]))
        .astype(jnp.bfloat16).reshape(seq_n, slots, qhalf)
    )
    parcel[:, :, qhalf:qhalf + vhalf] = (
        (dot(left, value_ref[:, 0:vhalf]) + dot(right, value_ref[:, vhalf:]))
        .astype(jnp.bfloat16).reshape(seq_n, slots, vhalf)
    )
    parcel[:, :, qhalf + vhalf:] = (
        dot(left + right, spot_ref[...]).astype(jnp.bfloat16).reshape(seq_n, slots, rows)
    )
    par = []
    for k in range(1, seq_n):
        to = lax.rem(s + k, seq_n)
        cp = remote(parcel.at[to], got.at[s], par_s.at[k], par_r.at[k], p, to)
        cp.start()
        par.append(cp)
    got[s] = parcel[s]
    target_out[s] = target_ref[...]
    cols_out[s] = cols_ref[s]

    if inside:
        cores = []

        def to_core(y, sh, slot):
            cp = remote(
                wall.at[y * 2 + cc, sh], wall.at[y * 2 + cc, sh], wc_s.at[slot], wc_r.at[slot],
                yb * 2 + 1 - cc, s,
            )
            cp.start()
            cores.append(cp)

        ys = []

        def to_y(sh, slot):
            for m in range(1, nb):
                cp = remote(
                    wall.at[p, sh], wall.at[p, sh], wy_s.at[m, slot], wy_r.at[m, slot],
                    lax.rem(yb + m, nb) * 2 + cc, s,
                )
                cp.start()
                ys.append((cp, m, slot))
            to_core(yb, sh, slot)

        xs = []
        for k in range(na):
            if k > 0:
                zc[k - 1].wait_recv()
            sh = lax.rem(a - k + na, na) * 2 + b
            cp = remote(wall.at[p, sh], wall.at[p, sh], wx_s.at[k], wx_r.at[k], p, a * 2 + 1 - b)
            cp.start()
            xs.append(cp)
            to_y(sh, 2 * k)
        for k in range(na):
            xs[k].wait_recv()
            to_y(lax.rem(a - k + na, na) * 2 + 1 - b, 2 * k + 1)
        for cp, m, slot in ys:
            cp.wait_recv()
            k, other = slot // 2, slot % 2
            sh = lax.rem(a - k + na, na) * 2 + (1 - b if other else b)
            to_core(lax.rem(yb - m + nb, nb), sh, m * seq_n + slot)
        for cp in cores:
            cp.wait_recv()
        waits += zc + xs + [c[0] for c in ys] + cores
        weights = wall[...].reshape(hidden_ref.shape[1], -1)
    else:
        weights = w_ref[...]

    projected = dot(hidden_ref[...], weights)
    cosine = cos_ref[...]
    sine = sin_ref[...]
    keys = jnp.concatenate(
        [
            turned(projected[:, g * HEAD_DIM:(g + 1) * HEAD_DIM], cosine, sine)
            for g in range(kvn)
        ],
        axis=1,
    ).astype(jnp.bfloat16)
    kparcel[...] = (
        (dot(left, keys[:, 0:vhalf]) + dot(right, keys[:, vhalf:]))
        .astype(jnp.bfloat16).reshape(seq_n, slots, vhalf)
    )
    ks = []
    for k in range(1, seq_n):
        to = lax.rem(s + k, seq_n)
        cp = remote(kparcel.at[to], kgot.at[s], k_s.at[k], k_r.at[k], p, to)
        cp.start()
        ks.append(cp)
    for k in range(1, seq_n):
        to = lax.rem(s + k, seq_n)
        cp = remote(cols_ref.at[to], cols_out.at[s], col_s.at[k], col_r.at[k], p, to)
        cp.start()
        waits.append(cp)
        cp = remote(target_ref, target_out.at[s], tgt_s.at[k], tgt_r.at[k], p, to)
        cp.start()
        waits.append(cp)
    kgot[s] = kparcel[s]

    for cp in par:
        cp.wait_recv()
    marks = got[:, :, qhalf + vhalf:].reshape(seq_n * slots, rows)
    place = lax.rem(lax.broadcasted_iota(jnp.int32, marks.shape, 0), slots)
    first = jnp.where(place < cap, marks, jnp.zeros_like(marks))
    second = jnp.where(place < cap, jnp.zeros_like(marks), marks)
    for half, mark in ((0, first), (1, second)):
        base = half * (heads // 2)
        settled = dot(mark, got[:, :, 0:qhalf].reshape(seq_n * slots, qhalf), 0, 0).astype(
            jnp.bfloat16
        )
        for h in range(heads // 2):
            head = base + h
            q_out[head // group, (head % group) * rows:(head % group + 1) * rows, :] = settled[
                :, h * HEAD_DIM:(h + 1) * HEAD_DIM
            ]
        settled = dot(
            mark, got[:, :, qhalf:qhalf + vhalf].reshape(seq_n * slots, vhalf), 0, 0
        ).astype(jnp.bfloat16)
        for h in range(kvn // 2):
            kv_out[kvn + half * (kvn // 2) + h, SPAN * rows:, :] = settled[
                :, h * HEAD_DIM:(h + 1) * HEAD_DIM
            ]
    for cp in ks:
        cp.wait_recv()
    for half, mark in ((0, first), (1, second)):
        settled = dot(mark, kgot[...].reshape(seq_n * slots, vhalf), 0, 0).astype(jnp.bfloat16)
        for h in range(kvn // 2):
            kv_out[half * (kvn // 2) + h, SPAN * rows:, :] = settled[
                :, h * HEAD_DIM:(h + 1) * HEAD_DIM
            ]

    def shift(by):
        return remote(
            kv_out.at[:, SPAN * rows:(SPAN + 1) * rows, :],
            kv_out.at[:, (SPAN - by) * rows:(SPAN - by + 1) * rows, :],
            sh_s.at[by], sh_r.at[by], p, lax.rem(s + by, seq_n),
        )

    for by in range(1, SPAN + 1):
        @pl.when(s + by < seq_n)
        def _(by=by):
            shift(by).start()

        @pl.when(s < by)
        def _(by=by):
            kv_out[:, (SPAN - by) * rows:(SPAN - by + 1) * rows, :] = jnp.zeros(
                (2 * kvn, rows, HEAD_DIM), jnp.bfloat16
            )
    for cp in par + ks:
        cp.wait_send()
    if inside:
        for cp in zc + xs + [c[0] for c in ys] + cores:
            cp.wait_send()
        waits = waits[len(zc) + len(xs) + len(ys) + len(cores):]
    for cp in waits:
        cp.wait()
    for by in range(1, SPAN + 1):
        @pl.when(s + by < seq_n)
        def _(by=by):
            shift(by).wait_send()

        @pl.when(s >= by)
        def _(by=by):
            shift(by).wait_recv()


def attention_kernel(
    head_total, q_ref, k_ref, v_ref, pick_ref, prob_ref, start_ref, out_ref, loss_ref, grad_ref
):
    step = pl.program_id(0)
    scaling = HEAD_DIM ** (-0.5)
    queries = q_ref[0]
    width = k_ref.shape[1]
    lanes = queries.shape[0]
    rows = out_ref.shape[0]
    group = lanes // rows
    score = dot(k_ref[0], queries, 1, 1) * scaling
    spot = lax.broadcasted_iota(jnp.int32, (width, lanes), 0)
    last = lax.rem(lax.broadcasted_iota(jnp.int32, (1, lanes), 1), rows) + (width - rows)
    allowed = (spot >= start_ref[...]) & (spot <= last)
    held = jnp.where(allowed, score, negative)
    top = jnp.max(held, axis=0, keepdims=True)
    raised = jnp.exp(held - top)
    total = jnp.sum(raised, axis=0, keepdims=True)
    lse = top + jnp.log(total)
    weight = raised * (1.0 / total)
    prob = prob_ref[0]
    table = jnp.zeros((width, lanes), jnp.float32)
    for k in range(prob.shape[0]):
        table += jnp.where(spot == pick_ref[0, k:k + 1, :], prob[k:k + 1, :], 0.0)
    mass = jnp.sum(prob, axis=0, keepdims=True)
    entropy = jnp.sum(prob * jnp.log(prob), axis=0, keepdims=True)
    picked = jnp.sum(table * score, axis=0, keepdims=True)
    loss = (entropy - picked + mass * lse) / head_total
    part = loss[:, 0:rows]
    for h in range(1, group):
        part += loss[:, h * rows:(h + 1) * rows]

    @pl.when(step == 0)
    def _():
        loss_ref[...] = part

    @pl.when(step > 0)
    def _():
        loss_ref[...] += part

    output = dot(weight.astype(jnp.bfloat16), v_ref[0], 0, 0).astype(jnp.bfloat16)
    for h in range(group):
        out_ref[:, h * HEAD_DIM:(h + 1) * HEAD_DIM] = output[h * rows:(h + 1) * rows, :]
    slope = ((weight * mass - table) * (1.0 / head_total)).astype(jnp.bfloat16)
    grad_ref[...] = dot(slope, queries) * scaling


def gradient_kernel(
    seq_n, dp_n, scale,
    grad_ref, cos_ref, sin_ref, cols_ref, target_ref,
    out_ref,
    sent, back, sorted_cols, kg, share, arrived,
    b_s, b_r, z_s, z_r, x_s, x_r, d_s, d_r,
):
    s = lax.axis_index("seq")
    p = lax.axis_index("dp")
    rows = cos_ref.shape[0]
    a, b = s // 2, lax.rem(s, 2)
    na = seq_n // 2
    greet(seq_n, dp_n)
    for by in range(1, SPAN + 1):
        sent[by - 1] = grad_ref[(SPAN - by) * rows:(SPAN - by + 1) * rows, :].astype(jnp.bfloat16)

    def shift(by):
        return remote(
            sent.at[by - 1], back.at[by - 1], b_s.at[by], b_r.at[by], p,
            lax.rem(s - by + seq_n, seq_n),
        )

    for by in range(1, SPAN + 1):
        @pl.when(s >= by)
        def _(by=by):
            shift(by).start()

        @pl.when(s + by >= seq_n)
        def _(by=by):
            back[by - 1] = jnp.zeros(back.shape[1:], jnp.bfloat16)

    count = seq_n * rows
    total = jnp.zeros((count, cols_ref.shape[2]), jnp.float32)
    spot = lax.broadcasted_iota(jnp.int32, (count, rows), 0)
    for j in range(seq_n):
        hit = jnp.where(spot == target_ref[j, 0:1, :], 1.0, 0.0).astype(jnp.bfloat16)
        total += dot(hit, cols_ref[j])
    sorted_cols[...] = total.astype(jnp.bfloat16).reshape(sorted_cols.shape)

    for by in range(1, SPAN + 1):
        @pl.when(s + by < seq_n)
        def _(by=by):
            shift(by).wait_recv()
    rotated = grad_ref[SPAN * rows:, :]
    for by in range(1, SPAN + 1):
        rotated += back[by - 1].astype(jnp.float32)
    cosine = cos_ref[...]
    sine = -sin_ref[...]
    kg[s] = jnp.concatenate(
        [
            turned(rotated[:, g * HEAD_DIM:(g + 1) * HEAD_DIM], cosine, sine)
            for g in range(rotated.shape[1] // HEAD_DIM)
        ],
        axis=1,
    ).astype(jnp.bfloat16)
    zc, xs = [], []
    for k in range(1, na):
        cp = remote(kg.at[s], kg.at[s], z_s.at[k], z_r.at[k], p, lax.rem(a + k, na) * 2 + b)
        cp.start()
        zc.append(cp)
    result = None
    for k in range(na):
        if k > 0:
            zc[k - 1].wait_recv()
        sh = lax.rem(a - k + na, na) * 2 + b
        cp = remote(kg.at[sh], kg.at[sh], x_s.at[k], x_r.at[k], p, a * 2 + 1 - b)
        cp.start()
        xs.append(cp)
        term = dot(sorted_cols[sh], kg[sh], 0, 0)
        result = term if result is None else result + term
    for k in range(na):
        xs[k].wait_recv()
        sh = lax.rem(a - k + na, na) * 2 + 1 - b
        result += dot(sorted_cols[sh], kg[sh], 0, 0)
    result *= scale
    depth = share.shape[1]
    for m in range(dp_n):
        share[m] = result[m * depth:(m + 1) * depth, :].astype(share.dtype)
    ds = []
    for m in range(1, dp_n):
        to = lax.rem(p + m, dp_n)
        cp = remote(share.at[to], arrived.at[m], d_s.at[m], d_r.at[m], to, s)
        cp.start()
        ds.append(cp)
    final = share[p].astype(jnp.float32)
    for m in range(1, dp_n):
        ds[m - 1].wait_recv()
        final += arrived[m].astype(jnp.float32)
    out_ref[...] = final
    for cp in zc + xs + ds:
        cp.wait_send()
    for by in range(1, SPAN + 1):
        @pl.when(s >= by)
        def _(by=by):
            shift(by).wait_send()


def local(
    hidden, queries, values, row_target, key_weight, dialogue_lengths, teacher_pick, teacher_prob
):
    rows = hidden.shape[0]
    seq_n = lax.axis_size("seq")
    dp_n = lax.axis_size("dp")
    s = lax.axis_index("seq")
    depth, kv_width = key_weight.shape
    capacity = rows // seq_n + rows // (2 * seq_n)
    capacity = -(-capacity // 8) * 8
    heads = queries.shape[1] // HEAD_DIM
    kvn = kv_width // HEAD_DIM
    group = heads // kvn
    top = teacher_pick.shape[1] // heads
    slots = 2 * capacity
    vmem = pl.BlockSpec(memory_space=pltpu.VMEM)
    dma = pltpu.SemaphoreType.DMA
    bf16 = jnp.bfloat16

    destination = row_target // rows
    offset = row_target - destination * rows
    order = jnp.arange(rows, dtype=jnp.int32)
    earlier = (destination[None, :] == destination[:, None]) & (order[None, :] < order[:, None])
    rank = jnp.sum(earlier.astype(jnp.int32), axis=1)
    slot = destination * slots + rank
    every = jnp.arange(seq_n * slots, dtype=jnp.int32)[:, None]
    left = (every == slot[None, :]).astype(bf16)
    right = (every == slot[None, :] + capacity).astype(bf16)
    marks = (offset[:, None] == order[None, :]).astype(bf16)
    cos_row, sin_row = angles(row_target)
    columns = hidden.reshape(rows, dp_n, seq_n, depth).transpose(2, 0, 1, 3)
    columns = columns.reshape(seq_n, rows, dp_n * depth)
    target_tile = jnp.broadcast_to(row_target[None, :], (8, rows))

    inside = depth % 16 == 0
    weight_in = key_weight
    if not inside:
        weight_in = lax.all_gather(key_weight, ("dp", "seq"), axis=0, tiled=True)
    qhalf, vhalf = queries.shape[1] // 2, kv_width // 2
    na, nb = seq_n // 2, dp_n // 2
    wall = (dp_n, seq_n, depth, kv_width) if inside else (8, 128)
    pairs = [
        (na,), (na,), (na,), (na,), (nb, seq_n), (nb, seq_n), (nb * seq_n,), (nb * seq_n,),
    ] + [(seq_n,)] * 8 + [(SPAN + 1,)] * 2
    q_seq, kv_win, cols_all, target_all = pl.pallas_call(
        functools.partial(gather_kernel, seq_n, dp_n, inside),
        out_shape=(
            jax.ShapeDtypeStruct((kvn, group * rows, HEAD_DIM), bf16),
            jax.ShapeDtypeStruct((2 * kvn, (SPAN + 1) * rows, HEAD_DIM), bf16),
            jax.ShapeDtypeStruct(columns.shape, bf16),
            jax.ShapeDtypeStruct((seq_n, 8, rows), jnp.int32),
        ),
        in_specs=[vmem] * 11,
        out_specs=(vmem,) * 4,
        scratch_shapes=[
            pltpu.VMEM(wall, bf16),
            pltpu.VMEM((seq_n, slots, qhalf + vhalf + rows), bf16),
            pltpu.VMEM((seq_n, slots, qhalf + vhalf + rows), bf16),
            pltpu.VMEM((seq_n, slots, vhalf), bf16),
            pltpu.VMEM((seq_n, slots, vhalf), bf16),
        ] + [dma(shape) for shape in pairs],
        compiler_params=pltpu.CompilerParams(
            collective_id=0, has_side_effects=True, vmem_limit_bytes=VMEM_BYTES
        ),
    )(
        weight_in, hidden, queries, values, left, right, marks, cos_row, sin_row, columns,
        target_tile,
    )

    positions = s * rows + order
    ending = jnp.cumsum(dialogue_lengths[0])
    starts = jnp.sum(
        jnp.where(ending[None, :] <= positions[:, None], dialogue_lengths[0][None, :], 0), axis=1
    )
    base = (s - SPAN) * rows
    reach = (positions - starts + 1)[:, None]
    picks = (starts[:, None] - base + teacher_pick % reach).reshape(rows, kvn, group, top)
    picks = picks.transpose(1, 3, 2, 0).reshape(kvn, top, group * rows)
    probs = teacher_prob.reshape(rows, kvn, group, top).transpose(1, 3, 2, 0)
    probs = probs.reshape(kvn, top, group * rows)
    lower = jnp.tile(starts - base, group)[None, :]
    width = (SPAN + 1) * rows
    lanes = group * rows
    attn_out, loss, grads = pl.pallas_call(
        functools.partial(attention_kernel, heads),
        grid=(kvn,),
        out_shape=(
            jax.ShapeDtypeStruct((rows, heads * HEAD_DIM), bf16),
            jax.ShapeDtypeStruct((1, rows), jnp.float32),
            jax.ShapeDtypeStruct((width, kv_width), jnp.float32),
        ),
        in_specs=[
            pl.BlockSpec((1, lanes, HEAD_DIM), lambda g: (g, 0, 0)),
            pl.BlockSpec((1, width, HEAD_DIM), lambda g: (g, 0, 0)),
            pl.BlockSpec((1, width, HEAD_DIM), lambda g: (g + kvn, 0, 0)),
            pl.BlockSpec((1, top, lanes), lambda g: (g, 0, 0)),
            pl.BlockSpec((1, top, lanes), lambda g: (g, 0, 0)),
            pl.BlockSpec((1, lanes), lambda g: (0, 0)),
        ],
        out_specs=(
            pl.BlockSpec((rows, group * HEAD_DIM), lambda g: (0, g)),
            pl.BlockSpec((1, rows), lambda g: (0, 0)),
            pl.BlockSpec((width, HEAD_DIM), lambda g: (0, g)),
        ),
        compiler_params=pltpu.CompilerParams(vmem_limit_bytes=VMEM_BYTES),
    )(q_seq, kv_win, kv_win, picks, probs, lower)

    cos_pos, sin_pos = angles(positions)
    link = bf16 if depth % 16 == 0 else jnp.float32
    weight_grad = pl.pallas_call(
        functools.partial(
            gradient_kernel, seq_n, dp_n, (rows * seq_n * dp_n) ** (-0.5)
        ),
        out_shape=jax.ShapeDtypeStruct((depth, kv_width), jnp.float32),
        in_specs=[vmem] * 5,
        out_specs=vmem,
        scratch_shapes=[
            pltpu.VMEM((SPAN, rows, kv_width), bf16),
            pltpu.VMEM((SPAN, rows, kv_width), bf16),
            pltpu.VMEM((seq_n, rows, dp_n * depth), bf16),
            pltpu.VMEM((seq_n, rows, kv_width), bf16),
            pltpu.VMEM((dp_n, depth, kv_width), link),
            pltpu.VMEM((dp_n, depth, kv_width), link),
            dma((SPAN + 1,)), dma((SPAN + 1,)), dma((na,)), dma((na,)), dma((na,)), dma((na,)),
            dma((dp_n,)), dma((dp_n,)),
        ],
        compiler_params=pltpu.CompilerParams(
            collective_id=1, has_side_effects=True, vmem_limit_bytes=VMEM_BYTES
        ),
    )(grads, cos_pos, sin_pos, cols_all, target_all)
    return attn_out, loss[0], weight_grad


def solution(mesh):
    both = P(("dp", "seq"), None)
    flat = P(("dp", "seq"))
    return jax.shard_map(
        local,
        mesh=mesh,
        in_specs=(both, both, both, flat, both, P("dp", None), both, both),
        out_specs=(both, flat, both),
        check_vma=False,
    )
```

time: 275 us -> 110 us (0.40)
  the two profiles are of different devices: /device:TPU:0 before, /device:TPU:21 now
where the time goes in v1:
time: 110 us
  Pallas kernels  101 us (92%)
  local copies, waits for them, and re-layouts  4.41 us (4%)
  other arithmetic  2.87 us (3%)
    pallas_call x1, Pallas kernels, local(): pl.pallas_call(functools.partial(gather_kernel, seq_n, dp_n, inside), out...  55.4 us
    pallas_call x1, Pallas kernels, local(): pl.pallas_call(functools.partial(gradient_kernel, seq_n, dp_n, (rows * se...  38.5 us
    pallas_call x1, Pallas kernels, local(): pl.pallas_call(functools.partial(attention_kernel, heads), grid=(kvn,), o...  7.54 us
    unnamed x18, local copies, waits for them, and re-layouts  2.75 us

profile of v1, /device:TPU:21, one launch (start us, length us, event | category | flops | bytes accessed | tf_op | source)
XLA Modules:
  0.0 109.6 jit_solution(18218814830271957866)
XLA Ops:
  0.7 0.7 multiply_subtract_fusion
  1.4 0.2 convert_reduce_fusion
  1.6 0.7 broadcast_in_dim.13.target_ref
  2.3 0.7 copy.24
  3.0 0.1 reduce
  3.2 0.5 copy-done.6
  3.7 0.1 select_reduce_fusion
  3.8 0.1 fusion.4.spot_ref
  3.9 0.1 copy.25
  4.0 0.7 fusion.2
  4.7 0.2 copy-done.5
  4.8 0.1 copy.26
  5.0 0.5 fusion.6
  5.6 0.1 pad_maximum_fusion.3.sin_ref
  5.6 0.1 pad_maximum_fusion.2.cos_ref
  5.8 0.1 pad_maximum_fusion.1.sin_ref
  5.9 0.1 copy-done
  6.0 0.3 copy.21
  6.4 0.2 copy.23.cols_ref
  6.6 0.8 copy-done.1
  7.4 55.4 %shard_map.103 = (bf16[4,512,128]{2,1,0:T(8,128)(2,1)S(1)}, bf16[8,384,128]{2,1,0:T(8,128)(2,1)S(1)}, bf16[8,128,256]{2,1,0:T(8,128)(2,1)S(1)}, s32[8,8,128]{2,1,0:T(8,128)S(1)}) custom-call(bf16[64,512]{1,0:T(8,128)(2,1)S(1)} %copy-done.3, bf16[128,2048]{1,0:T(8,128)(2,1)S(1)} %copy-done, bf16[128,2048]{1,0:T(8,128)(2,1)S(1)} %copy-done.1, ...), custom_call_target="tpu_custom_call" | custom-call | tf_op jit(solution)/shard_map/pallas_call | solution.py:448
  62.9 7.5 %shard_map.104 = (bf16[128,2048]{1,0:T(8,128)(2,1)}, f32[1,128]{1,0:T(1,128)}, f32[384,512]{1,0:T(8,128)S(1)}) custom-call(bf16[4,512,128]{2,1,0:T(8,128)(2,1)S(1)} %get-tuple-element.10.q_ref, bf16[8,384,128]{2,1,0:T(8,128)(2,1)S(1)} %get-tuple-element.11.k_ref.v_ref, bf16[8,384,128]{2,1,0:T(8,128)(2,1)S(1)} %get-tuple-element.11.k_ref.v_ref, ...), custom_call_target="tpu_custom_call" | custom-call | tf_op jit(solution)/shard_map/pallas_call | solution.py:487
  70.4 38.5 %shard_map.105 = f32[64,512]{1,0:T(8,128)S(1)} custom-call(f32[384,512]{1,0:T(8,128)S(1)} %get-tuple-element.14.grad_ref, f32[128,128]{1,0:T(8,128)S(1)} %pad_maximum_fusion.2.cos_ref, f32[128,128]{1,0:T(8,128)S(1)} %pad_maximum_fusion.3.sin_ref, bf16[8,128,256]{2,1,0:T(8,128)(2,1)S(1)} %get-tuple-element.15.cols_ref, ...), custom_call_target="tpu_custom_call" | custom-call | tf_op jit(solution)/shard_map/pallas_call | solution.py:513
  108.9 0.7 copy.28
  (20 shorter events, 0.3 us)
Async XLA Ops:
  0.6 3.3 %copy-start.4 = (s32[128,128]{1,0:T(8,128)S(1)}, s32[128,128]{1,0:T(8,128)}, u32[]{:S(2)}) copy-start(s32[128,128]{1,0:T(8,128)} %param.14) | copy-start | bytes 196612
  3.0 0.7 copy-start.6
  4.0 0.8 copy-start.5
  5.0 1.0 copy-start
  6.4 1.0 copy-start.1
  6.4 1.1 copy-start.2
  6.4 1.0 copy-start.3

commit v2 on v1

v2 whole, which is shorter than its diff:
```python
import functools

import jax
import jax.numpy as jnp
from jax import lax
from jax.experimental import pallas as pl
from jax.experimental.pallas import tpu as pltpu
from jax.sharding import PartitionSpec as P

HEAD_DIM = 128
SPAN = 2
MESH = pl.DeviceIdType.MESH
VMEM_BYTES = 50 * 1024 * 1024

negative = -1e30
rope_base = 500000.0


def angles(positions):
    halfway = HEAD_DIM // 2
    frequency = rope_base ** (-2.0 * jnp.arange(halfway, dtype=jnp.float32) / HEAD_DIM)
    angle = positions.astype(jnp.float32)[:, None] * frequency[None, :]
    cosine = jnp.cos(angle)
    sine = jnp.sin(angle)
    return (
        jnp.concatenate([cosine, cosine], axis=1),
        jnp.concatenate([-sine, sine], axis=1),
    )


def turned(block, cosine, sine):
    return block * cosine + pltpu.roll(block, HEAD_DIM // 2, 1) * sine


def dot(a, b, ca=1, cb=0):
    return lax.dot_general(a, b, (((ca,), (cb,)), ((), ())), preferred_element_type=jnp.float32)


def greet(seq_n, dp_n):
    s = lax.axis_index("seq")
    p = lax.axis_index("dp")
    barrier = pltpu.get_barrier_semaphore()
    for k in range(1, seq_n):
        pl.semaphore_signal(
            barrier, inc=1, device_id=(p, lax.rem(s + k, seq_n)), device_id_type=MESH
        )
    for k in range(1, dp_n):
        pl.semaphore_signal(
            barrier, inc=1, device_id=(lax.rem(p + k, dp_n), s), device_id_type=MESH
        )
    pl.semaphore_wait(barrier, seq_n - 1 + dp_n - 1)


def remote(src, dst, send, recv, p, s):
    return pltpu.make_async_remote_copy(
        src_ref=src, dst_ref=dst, send_sem=send, recv_sem=recv, device_id=(p, s),
        device_id_type=MESH,
    )


def mirror(a, size):
    return (a // size) * size * 2 + size - 1 - a


def mirror_prefix(a, levels, stop):
    held = [a]
    for size in levels:
        if size == stop:
            return held
        held = held + mirror_prefix(mirror(a, size), levels, size)
    return held


def spread(levels, a, peer, send, recv, place, on_hold):
    copies = []
    on_hold(a, 0)
    count = 1
    for size in levels:
        partner = mirror(a, size)
        mine = mirror_prefix(a, levels, size)
        theirs = mirror_prefix(partner, levels, size)
        fresh = []
        for i, shard in enumerate(mine):
            cp = remote(
                place(shard), place(shard), send.at[count + i], recv.at[count + i], *peer(partner)
            )
            cp.start()
            fresh.append(cp)
        for i, shard in enumerate(theirs):
            fresh[i].wait_recv()
            on_hold(shard, count + i)
        copies += fresh
        count += len(mine)
    return copies


def whole_kernel(
    seq_n, dp_n, inside, scale,
    w_ref, hidden_ref, query_ref, value_ref, left_ref, right_ref, cos_ref, sin_ref,
    cols_ref, target_ref, pick_ref, prob_ref, start_ref, cospos_ref, sinpos_ref,
    att_ref, loss_ref, out_ref,
    wall, parcel, got, kparcel, kgot, marks_ref, q_seq, kv_win, cols_all, target_all,
    own, sent, back, sorted_cols, kg, share, arrived,
    wz_s, wz_r, wx_s, wx_r, wy_s, wy_r, wc_s, wc_r,
    par_s, par_r, col_s, col_r, tgt_s, tgt_r, k_s, k_r, sh_s, sh_r,
    b_s, b_r, z_s, z_r, x_s, x_r, d_s, d_r,
):
    s = lax.axis_index("seq")
    p = lax.axis_index("dp")
    rows = query_ref.shape[0]
    qhalf = query_ref.shape[1] // 2
    vhalf = value_ref.shape[1] // 2
    kvn = value_ref.shape[1] // HEAD_DIM
    heads = query_ref.shape[1] // HEAD_DIM
    group = heads // kvn
    slots = got.shape[1]
    cap = slots // 2
    a, b = s // 2, lax.rem(s, 2)
    yb, cc = p // 2, lax.rem(p, 2)
    na, nb = seq_n // 2, dp_n // 2
    levels = []
    while (na >> len(levels)) > 1:
        levels.append(na >> len(levels))
    if inside:
        wall[p, s] = w_ref[...]
    greet(seq_n, dp_n)
    sends = []

    def others():
        return [(k, lax.rem(s + k, seq_n)) for k in range(1, seq_n)]

    tgts = []
    for k, to in others():
        cp = remote(target_ref, target_all.at[s], tgt_s.at[k], tgt_r.at[k], p, to)
        cp.start()
        tgts.append(cp)
    target_all[s] = target_ref[...]

    left = left_ref[...]
    right = right_ref[...]

    def send_queries():
        parcel[...] = (
            (dot(left, query_ref[:, 0:qhalf]) + dot(right, query_ref[:, qhalf:]))
            .astype(jnp.bfloat16).reshape(seq_n, slots, qhalf)
        )
        started = []
        for k, to in others():
            cp = remote(parcel.at[to], got.at[s], par_s.at[k], par_r.at[k], p, to)
            cp.start()
            started.append(cp)
        got[s] = parcel[s]
        kparcel[:, :, vhalf:] = (
            (dot(left, value_ref[:, 0:vhalf]) + dot(right, value_ref[:, vhalf:]))
            .astype(jnp.bfloat16).reshape(seq_n, slots, vhalf)
        )
        return started

    par = []
    if inside:
        cores, ys, xs = [], [], []

        def to_core(y, sh, slot):
            where = wall.at[y * 2 + cc, sh]
            cp = remote(where, where, wc_s.at[slot], wc_r.at[slot], yb * 2 + 1 - cc, s)
            cp.start()
            cores.append(cp)

        def to_y(sh, slot):
            for m in range(1, nb):
                where = wall.at[p, sh]
                cp = remote(
                    where, where, wy_s.at[m, slot], wy_r.at[m, slot],
                    lax.rem(yb + m, nb) * 2 + cc, s,
                )
                cp.start()
                ys.append((cp, m, slot, sh))
            to_core(yb, sh, slot)

        def held_w(shard, index):
            sh = shard * 2 + b
            cp = remote(
                wall.at[p, sh], wall.at[p, sh], wx_s.at[index], wx_r.at[index], p, a * 2 + 1 - b
            )
            cp.start()
            xs.append((cp, index, shard * 2 + 1 - b))
            to_y(sh, 2 * index)

        zc = spread(
            levels, a, lambda t: (p, t * 2 + b), wz_s, wz_r,
            lambda shard: wall.at[p, shard * 2 + b], held_w,
        )
        par = send_queries()
        for cp, index, sh in xs:
            cp.wait_recv()
            to_y(sh, 2 * index + 1)
        for cp, m, slot, sh in list(ys):
            cp.wait_recv()
            to_core(lax.rem(yb - m + nb, nb), sh, m * seq_n + slot)
        for cp in cores:
            cp.wait_recv()
        sends += zc + [c[0] for c in xs] + [c[0] for c in ys] + cores
        weights = wall[...].reshape(hidden_ref.shape[1], -1)
    else:
        par = send_queries()
        weights = w_ref[...]

    projected = dot(hidden_ref[...], weights)
    cosine = cos_ref[...]
    sine = sin_ref[...]
    keys = jnp.concatenate(
        [
            turned(projected[:, g * HEAD_DIM:(g + 1) * HEAD_DIM], cosine, sine)
            for g in range(kvn)
        ],
        axis=1,
    ).astype(jnp.bfloat16)
    kparcel[:, :, 0:vhalf] = (
        (dot(left, keys[:, 0:vhalf]) + dot(right, keys[:, vhalf:]))
        .astype(jnp.bfloat16).reshape(seq_n, slots, vhalf)
    )
    ks = []
    for k, to in others():
        cp = remote(kparcel.at[to], kgot.at[s], k_s.at[k], k_r.at[k], p, to)
        cp.start()
        ks.append(cp)
    kgot[s] = kparcel[s]

    for cp in tgts:
        cp.wait_recv()
    square = (rows, rows)
    down = lax.broadcasted_iota(jnp.int32, square, 0)
    across = lax.broadcasted_iota(jnp.int32, square, 1)
    before = jnp.where(down < across, 1.0, 0.0).astype(jnp.bfloat16)
    slot_id = lax.broadcasted_iota(jnp.int32, (slots, rows), 0)
    slot_id = jnp.where(slot_id >= cap, slot_id - cap, slot_id).astype(jnp.float32)
    for j in range(seq_n):
        offset = target_all[j] - s * rows
        mine = (offset >= 0) & (offset < rows)
        flag = jnp.where(mine, 1.0, 0.0)
        rank = dot(flag.astype(jnp.bfloat16), before)
        rank = jnp.where(mine, rank, -1.0)
        filled = jnp.where(slot_id == rank[0:1, :], 1.0, 0.0).astype(jnp.bfloat16)
        at = jnp.where(down == offset[0:1, :], 1.0, 0.0).astype(jnp.bfloat16)
        marks_ref[j] = dot(filled, at, 1, 1).astype(jnp.bfloat16)
    marks = marks_ref[...].reshape(seq_n * slots, rows)
    place = lax.rem(lax.broadcasted_iota(jnp.int32, marks.shape, 0), slots)
    first = jnp.where(place < cap, marks, jnp.zeros_like(marks))
    second = jnp.where(place < cap, jnp.zeros_like(marks), marks)

    for cp in par:
        cp.wait_recv()
    for half, mark in ((0, first), (1, second)):
        base = half * (heads // 2)
        settled = dot(mark, got[...].reshape(seq_n * slots, qhalf), 0, 0).astype(jnp.bfloat16)
        for h in range(heads // 2):
            head = base + h
            q_seq[head // group, (head % group) * rows:(head % group + 1) * rows, :] = settled[
                :, h * HEAD_DIM:(h + 1) * HEAD_DIM
            ]
    for cp in ks:
        cp.wait_recv()
    for half, mark in ((0, first), (1, second)):
        settled = dot(mark, kgot[...].reshape(seq_n * slots, 2 * vhalf), 0, 0).astype(jnp.bfloat16)
        for h in range(kvn):
            head = (h // (kvn // 2)) * kvn + half * (kvn // 2) + h % (kvn // 2)
            kv_win[head, SPAN * rows:, :] = settled[:, h * HEAD_DIM:(h + 1) * HEAD_DIM]

    def shift(by):
        return remote(
            kv_win.at[:, SPAN * rows:(SPAN + 1) * rows, :],
            kv_win.at[:, (SPAN - by) * rows:(SPAN - by + 1) * rows, :],
            sh_s.at[by], sh_r.at[by], p, lax.rem(s + by, seq_n),
        )

    for by in range(1, SPAN + 1):
        @pl.when(s + by < seq_n)
        def _(by=by):
            shift(by).start()

        @pl.when(s < by)
        def _(by=by):
            kv_win[:, (SPAN - by) * rows:(SPAN - by + 1) * rows, :] = jnp.zeros(
                (2 * kvn, rows, HEAD_DIM), jnp.bfloat16
            )

        @pl.when(s + by >= seq_n)
        def _(by=by):
            back[by - 1] = jnp.zeros(back.shape[1:], jnp.bfloat16)
    cols = []
    for k, to in others():
        cp = remote(cols_ref.at[to], cols_all.at[s], col_s.at[k], col_r.at[k], p, to)
        cp.start()
        cols.append(cp)
    cols_all[s] = cols_ref[s]
    for by in range(1, SPAN + 1):
        @pl.when(s >= by)
        def _(by=by):
            shift(by).wait_recv()

    width = (SPAN + 1) * rows
    lanes = group * rows
    scaling = HEAD_DIM ** (-0.5)
    loss_ref[...] = jnp.zeros(loss_ref.shape, jnp.float32)

    def give(by, g):
        return remote(
            sent.at[by - 1, g], back.at[by - 1, g], b_s.at[by - 1, g], b_r.at[by - 1, g], p,
            lax.rem(s - by + seq_n, seq_n),
        )

    def attend(g, carry):
        queries = q_seq[g]
        score = dot(kv_win[g], queries, 1, 1) * scaling
        spot = lax.broadcasted_iota(jnp.int32, (width, lanes), 0)
        last = lax.rem(lax.broadcasted_iota(jnp.int32, (1, lanes), 1), rows) + (width - rows)
        allowed = (spot >= start_ref[...]) & (spot <= last)
        held = jnp.where(allowed, score, negative)
        top = jnp.max(held, axis=0, keepdims=True)
        raised = jnp.exp(held - top)
        total = jnp.sum(raised, axis=0, keepdims=True)
        lse = top + jnp.log(total)
        weight = raised * (1.0 / total)
        prob = prob_ref[g]
        pick = pick_ref[g]
        table = jnp.zeros((width, lanes), jnp.float32)
        for k in range(prob.shape[0]):
            table += jnp.where(spot == pick[k:k + 1, :], prob[k:k + 1, :], 0.0)
        mass = jnp.sum(prob, axis=0, keepdims=True)
        entropy = jnp.sum(prob * jnp.log(prob), axis=0, keepdims=True)
        picked = jnp.sum(table * score, axis=0, keepdims=True)
        loss = (entropy - picked + mass * lse) * (1.0 / heads)
        part = loss[:, 0:rows]
        for h in range(1, group):
            part += loss[:, h * rows:(h + 1) * rows]
        loss_ref[...] += part
        slope = ((weight * mass - table) * (1.0 / heads)).astype(jnp.bfloat16)
        grad = dot(slope, queries) * scaling
        own[g] = grad[SPAN * rows:, :]
        for by in range(1, SPAN + 1):
            sent[by - 1, g] = grad[(SPAN - by) * rows:(SPAN - by + 1) * rows, :].astype(
                jnp.bfloat16
            )

            @pl.when(s >= by)
            def _(by=by):
                give(by, g).start()

        output = dot(weight.astype(jnp.bfloat16), kv_win[kvn + g], 0, 0).astype(jnp.bfloat16)
        for h in range(group):
            lane = pl.multiple_of((g * group + h) * HEAD_DIM, HEAD_DIM)
            att_ref[:, pl.ds(lane, HEAD_DIM)] = output[h * rows:(h + 1) * rows, :]
        return carry

    lax.fori_loop(0, kvn, attend, 0)

    for cp in cols:
        cp.wait_recv()
    count = seq_n * rows
    total = jnp.zeros((count, cols_ref.shape[2]), jnp.float32)
    spot = lax.broadcasted_iota(jnp.int32, (count, rows), 0)
    for j in range(seq_n):
        hit = jnp.where(spot == target_all[j, 0:1, :], 1.0, 0.0).astype(jnp.bfloat16)
        total += dot(hit, cols_all[j])
    sorted_cols[...] = total.astype(jnp.bfloat16).reshape(sorted_cols.shape)

    for by in range(1, SPAN + 1):
        @pl.when(s + by < seq_n)
        def _(by=by):
            for g in range(kvn):
                give(by, g).wait_recv()
    cosine = cospos_ref[...]
    sine = -sinpos_ref[...]
    for g in range(kvn):
        rotated = own[g]
        for by in range(1, SPAN + 1):
            rotated += back[by - 1, g].astype(jnp.float32)
        kg[s, :, g * HEAD_DIM:(g + 1) * HEAD_DIM] = turned(rotated, cosine, sine).astype(
            jnp.bfloat16
        )
    pairs = []
    terms = []

    def held_kg(shard, index):
        sh = shard * 2 + b
        cp = remote(kg.at[sh], kg.at[sh], x_s.at[index], x_r.at[index], p, a * 2 + 1 - b)
        cp.start()
        pairs.append((cp, shard * 2 + 1 - b))
        terms.append(sh)

    zk = spread(
        levels, a, lambda t: (p, t * 2 + b), z_s, z_r, lambda shard: kg.at[shard * 2 + b], held_kg
    )
    result = None
    for sh in terms:
        term = dot(sorted_cols[sh], kg[sh], 0, 0)
        result = term if result is None else result + term
    for cp, sh in pairs:
        cp.wait_recv()
        result += dot(sorted_cols[sh], kg[sh], 0, 0)
    result *= scale
    depth = share.shape[1]
    for m in range(dp_n):
        share[m] = result[m * depth:(m + 1) * depth, :].astype(share.dtype)
    ds = []
    for m in range(1, dp_n):
        to = lax.rem(p + m, dp_n)
        cp = remote(share.at[to], arrived.at[m], d_s.at[m], d_r.at[m], to, s)
        cp.start()
        ds.append(cp)
    final = share[p].astype(jnp.float32)
    for m in range(1, dp_n):
        ds[m - 1].wait_recv()
        final += arrived[m].astype(jnp.float32)
    out_ref[...] = final
    for cp in sends + tgts + par + ks + cols + zk + [c[0] for c in pairs] + ds:
        cp.wait_send()
    for by in range(1, SPAN + 1):
        @pl.when(s + by < seq_n)
        def _(by=by):
            shift(by).wait_send()

        @pl.when(s >= by)
        def _(by=by):
            for g in range(kvn):
                give(by, g).wait_send()


def local(
    hidden, queries, values, row_target, key_weight, dialogue_lengths, teacher_pick, teacher_prob
):
    rows = hidden.shape[0]
    seq_n = lax.axis_size("seq")
    dp_n = lax.axis_size("dp")
    s = lax.axis_index("seq")
    depth, kv_width = key_weight.shape
    capacity = rows // seq_n + rows // (2 * seq_n)
    capacity = -(-capacity // 8) * 8
    heads = queries.shape[1] // HEAD_DIM
    kvn = kv_width // HEAD_DIM
    group = heads // kvn
    top = teacher_pick.shape[1] // heads
    slots = 2 * capacity
    vmem = pl.BlockSpec(memory_space=pltpu.VMEM)
    dma = pltpu.SemaphoreType.DMA
    bf16 = jnp.bfloat16

    destination = row_target // rows
    order = jnp.arange(rows, dtype=jnp.int32)
    earlier = (destination[None, :] == destination[:, None]) & (order[None, :] < order[:, None])
    rank = jnp.sum(earlier.astype(jnp.int32), axis=1)
    slot = destination * slots + rank
    every = jnp.arange(seq_n * slots, dtype=jnp.int32)[:, None]
    left = (every == slot[None, :]).astype(bf16)
    right = (every == slot[None, :] + capacity).astype(bf16)
    cos_row, sin_row = angles(row_target)
    columns = hidden.reshape(rows, dp_n, seq_n, depth).transpose(2, 0, 1, 3)
    columns = columns.reshape(seq_n, rows, dp_n * depth)
    target_tile = jnp.broadcast_to(row_target[None, :], (8, rows))

    positions = s * rows + order
    ending = jnp.cumsum(dialogue_lengths[0])
    starts = jnp.sum(
        jnp.where(ending[None, :] <= positions[:, None], dialogue_lengths[0][None, :], 0), axis=1
    )
    base = (s - SPAN) * rows
    reach = (positions - starts + 1)[:, None]
    picks = (starts[:, None] - base + teacher_pick % reach).reshape(rows, kvn, group, top)
    picks = picks.transpose(1, 3, 2, 0).reshape(kvn, top, group * rows)
    probs = teacher_prob.reshape(rows, kvn, group, top).transpose(1, 3, 2, 0)
    probs = probs.reshape(kvn, top, group * rows)
    lower = jnp.tile(starts - base, group)[None, :]
    cos_pos, sin_pos = angles(positions)

    inside = depth % 16 == 0
    weight_in = key_weight
    if not inside:
        weight_in = lax.all_gather(key_weight, ("dp", "seq"), axis=0, tiled=True)
    qhalf = queries.shape[1] // 2
    na, nb = seq_n // 2, dp_n // 2
    wall = (dp_n, seq_n, depth, kv_width) if inside else (8, 128)
    link = bf16 if inside else jnp.float32
    semaphores = (
        [(na,)] * 4 + [(nb, seq_n)] * 2 + [(nb * seq_n,)] * 2 + [(seq_n,)] * 8 + [(SPAN + 1,)] * 2
        + [(SPAN, kvn)] * 2 + [(na,)] * 4 + [(dp_n,)] * 2
    )
    attn_out, loss, weight_grad = pl.pallas_call(
        functools.partial(
            whole_kernel, seq_n, dp_n, inside, (rows * seq_n * dp_n) ** (-0.5)
        ),
        out_shape=(
            jax.ShapeDtypeStruct((rows, heads * HEAD_DIM), bf16),
            jax.ShapeDtypeStruct((1, rows), jnp.float32),
            jax.ShapeDtypeStruct((depth, kv_width), jnp.float32),
        ),
        in_specs=[vmem] * 15,
        out_specs=(vmem,) * 3,
        scratch_shapes=[
            pltpu.VMEM(wall, bf16),
            pltpu.VMEM((seq_n, slots, qhalf), bf16),
            pltpu.VMEM((seq_n, slots, qhalf), bf16),
            pltpu.VMEM((seq_n, slots, kv_width), bf16),
            pltpu.VMEM((seq_n, slots, kv_width), bf16),
            pltpu.VMEM((seq_n, slots, rows), bf16),
            pltpu.VMEM((kvn, group * rows, HEAD_DIM), bf16),
            pltpu.VMEM((2 * kvn, (SPAN + 1) * rows, HEAD_DIM), bf16),
            pltpu.VMEM(columns.shape, bf16),
            pltpu.VMEM((seq_n, 8, rows), jnp.int32),
            pltpu.VMEM((kvn, rows, HEAD_DIM), jnp.float32),
            pltpu.VMEM((SPAN, kvn, rows, HEAD_DIM), bf16),
            pltpu.VMEM((SPAN, kvn, rows, HEAD_DIM), bf16),
            pltpu.VMEM((seq_n, rows, dp_n * depth), bf16),
            pltpu.VMEM((seq_n, rows, kv_width), bf16),
            pltpu.VMEM((dp_n, depth, kv_width), link),
            pltpu.VMEM((dp_n, depth, kv_width), link),
        ] + [dma(shape) for shape in semaphores],
        compiler_params=pltpu.CompilerParams(
            collective_id=0, has_side_effects=True, vmem_limit_bytes=VMEM_BYTES
        ),
    )(
        weight_in, hidden, queries, values, left, right, cos_row, sin_row, columns, target_tile,
        picks, probs, lower, cos_pos, sin_pos,
    )
    return attn_out, loss[0], weight_grad


def solution(mesh):
    both = P(("dp", "seq"), None)
    flat = P(("dp", "seq"))
    return jax.shard_map(
        local,
        mesh=mesh,
        in_specs=(both, both, both, flat, both, P("dp", None), both, both),
        out_specs=(both, flat, both),
        check_vma=False,
    )
```

time: 110 us -> 99.3 us (0.903)
  the two profiles are of different devices: /device:TPU:21 before, /device:TPU:0 now
where the time goes in v2:
time: 99.3 us; the launch traced here: 97.8 us
  Pallas kernels  88.5 us (89%)
  local copies, waits for them, and re-layouts  5.71 us (6%)
  other arithmetic  2.78 us (3%)
    pallas_call x1, Pallas kernels, local(): pl.pallas_call(functools.partial(whole_kernel, seq_n, dp_n, inside, (rows...  88.5 us
    unnamed x20, local copies, waits for them, and re-layouts  4.06 us

profile of v2, /device:TPU:0, one launch (start us, length us, event | category | flops | bytes accessed | tf_op | source)
XLA Modules:
  0.0 97.8 jit_solution(9450282159104761749)
XLA Ops:
  0.7 0.7 fusion.7
  1.4 0.2 convert_reduce_fusion
  1.6 0.7 broadcast_in_dim.13.target_ref
  2.3 0.7 copy.23
  3.0 0.1 reduce
  3.2 0.5 copy-done.6
  3.7 0.1 select_reduce_fusion
  3.8 0.1 copy.24
  3.9 0.7 fusion.2
  4.6 0.2 copy-done.5
  4.8 0.1 copy.25
  4.9 0.5 fusion.5
  5.5 0.1 pad_maximum_fusion.3.sinpos_ref
  5.6 0.1 pad_maximum_fusion.2.cospos_ref
  5.6 0.1 pad_maximum_fusion.cos_ref
  5.7 0.1 pad_maximum_fusion.1.sin_ref
  5.8 0.1 copy-done
  6.0 0.3 copy.21
  6.3 0.2 copy.26.cols_ref
  6.5 0.8 copy-done.1
  7.3 88.5 %shard_map.103 = (bf16[128,2048]{1,0:T(8,128)(2,1)S(1)}, f32[1,128]{1,0:T(1,128)S(1)}, f32[64,512]{1,0:T(8,128)S(1)}) custom-call(bf16[64,512]{1,0:T(8,128)(2,1)S(1)} %copy-done.3, bf16[128,2048]{1,0:T(8,128)(2,1)S(1)} %copy-done, bf16[128,2048]{1,0:T(8,128)(2,1)S(1)} %copy-done.1, bf16[128,512]{1,0:T(8,128)(2,1)S(1)} %copy-done.2, ...), custom_call_target="tpu_custom_call" | custom-call | tf_op jit(solution)/shard_map/pallas_call | solution.py:487
  95.8 0.8 copy.30
  96.6 0.5 copy.31
  97.1 0.7 copy.32
  (19 shorter events, 0.2 us)
Async XLA Ops:
  0.6 3.2 %copy-start.4 = (s32[128,128]{1,0:T(8,128)S(1)}, s32[128,128]{1,0:T(8,128)}, u32[]{:S(2)}) copy-start(s32[128,128]{1,0:T(8,128)} %param.14) | copy-start | bytes 196612
  3.0 0.7 copy-start.6
  3.9 0.8 copy-start.5
  4.9 1.0 %copy-start = (bf16[128,2048]{1,0:T(8,128)(2,1)S(1)}, bf16[128,2048]{1,0:T(8,128)(2,1)}, u32[]{:S(2)}) copy-start(bf16[128,2048]{1,0:T(8,128)(2,1)} %hidden_ref.1) | copy-start | bytes 1572868
  6.3 1.0 %copy-start.1 = (bf16[128,2048]{1,0:T(8,128)(2,1)S(1)}, bf16[128,2048]{1,0:T(8,128)(2,1)}, u32[]{:S(2)}) copy-start(bf16[128,2048]{1,0:T(8,128)(2,1)} %query_ref.1) | copy-start | bytes 1572868
  6.3 1.1 %copy-start.2 = (bf16[128,512]{1,0:T(8,128)(2,1)S(1)}, bf16[128,512]{1,0:T(8,128)(2,1)}, u32[]{:S(2)}) copy-start(bf16[128,512]{1,0:T(8,128)(2,1)} %value_ref.1) | copy-start | bytes 393220
  6.3 1.0 %copy-start.3 = (bf16[64,512]{1,0:T(8,128)(2,1)S(1)}, bf16[64,512]{1,0:T(8,128)(2,1)}, u32[]{:S(2)}) copy-start(bf16[64,512]{1,0:T(8,128)(2,1)} %w_ref.1) | copy-start | bytes 196612

commit v3 on v2

--- a/solution.py
+++ b/solution.py
@@ -48,7 +48,7 @@
         pl.semaphore_signal(
             barrier, inc=1, device_id=(lax.rem(p + k, dp_n), s), device_id_type=MESH
         )
-    pl.semaphore_wait(barrier, seq_n - 1 + dp_n - 1)
+    return barrier
 
 
 def remote(src, dst, send, recv, p, s):
@@ -96,13 +96,13 @@
 
 def whole_kernel(
     seq_n, dp_n, inside, scale,
-    w_ref, hidden_ref, query_ref, value_ref, left_ref, right_ref, cos_ref, sin_ref,
-    cols_ref, target_ref, pick_ref, prob_ref, start_ref, cospos_ref, sinpos_ref,
+    w_ref, hidden_ref, query_ref, value_ref, row_ref, cos_ref, sin_ref,
+    cols_ref, drawn_ref, given_ref, lower_ref, cospos_ref, sinpos_ref,
     att_ref, loss_ref, out_ref,
-    wall, parcel, got, kparcel, kgot, marks_ref, q_seq, kv_win, cols_all, target_all,
+    wall, parcel, got, vparcel, vgot, kparcel, kgot, target_ref, pick_ref, prob_ref, marks_ref, q_seq, kv_win, cols_all, target_all,
     own, sent, back, sorted_cols, kg, share, arrived,
     wz_s, wz_r, wx_s, wx_r, wy_s, wy_r, wc_s, wc_r,
-    par_s, par_r, col_s, col_r, tgt_s, tgt_r, k_s, k_r, sh_s, sh_r,
+    par_s, par_r, v_s, v_r, col_s, col_r, tgt_s, tgt_r, k_s, k_r, sh_s, sh_r,
     b_s, b_r, z_s, z_r, x_s, x_r, d_s, d_r,
 ):
     s = lax.axis_index("seq")
@@ -121,42 +121,97 @@
     levels = []
     while (na >> len(levels)) > 1:
         levels.append(na >> len(levels))
+    barrier = greet(seq_n, dp_n)
     if inside:
         wall[p, s] = w_ref[...]
-    greet(seq_n, dp_n)
+    target_ref[...] = jnp.broadcast_to(row_ref[...], target_ref.shape)
     sends = []
 
     def others():
         return [(k, lax.rem(s + k, seq_n)) for k in range(1, seq_n)]
 
     tgts = []
+    target_all[s] = target_ref[...]
+
+    square = (rows, rows)
+    down = lax.broadcasted_iota(jnp.int32, square, 0)
+    across = lax.broadcasted_iota(jnp.int32, square, 1)
+    before = jnp.where(down < across, 1.0, 0.0).astype(jnp.bfloat16)
+
+    def packers():
+        target = row_ref[...]
+        block = lax.broadcasted_iota(jnp.int32, (seq_n, rows), 0) * rows
+        here = jnp.where((target >= block) & (target < block + rows), 1.0, 0.0)
+        seen = dot(here.astype(jnp.bfloat16), before)
+        index = lax.broadcasted_iota(jnp.int32, (seq_n, rows), 0).astype(jnp.float32)
+        slot = jnp.sum(here * (seen + index * slots), axis=0, keepdims=True)
+        every = lax.broadcasted_iota(jnp.int32, (seq_n * slots, rows), 0).astype(jnp.float32)
+        return (
+            jnp.where(every == slot, 1.0, 0.0).astype(jnp.bfloat16),
+            jnp.where(every == slot + cap, 1.0, 0.0).astype(jnp.bfloat16),
+        )
+
+    lower = lower_ref[...]
+    top_n = drawn_ref.shape[1] // heads
+
+    def labels():
+        lane = lax.broadcasted_iota(jnp.int32, (1, rows), 1)
+        reach = (lane + SPAN * rows - lower + 1).astype(jnp.float32)
+        drawn = jnp.transpose(drawn_ref[...].astype(jnp.float32))
+        left_over = drawn - jnp.floor(drawn * (1.0 / reach)) * reach
+        left_over = jnp.where(left_over < 0.0, left_over + reach, left_over)
+        left_over = jnp.where(left_over >= reach, left_over - reach, left_over)
+        chosen = left_over.astype(jnp.int32) + lower
+        given = jnp.transpose(given_ref[...])
+        for h in range(heads):
+            place = slice((h % group) * rows, (h % group + 1) * rows)
+            pick_ref[h // group, :, place] = chosen[h * top_n:(h + 1) * top_n, :]
+            prob_ref[h // group, :, place] = given[h * top_n:(h + 1) * top_n, :]
+
+    def places():
+        for cp in tgts:
+            cp.wait_recv()
+        slot_id = lax.broadcasted_iota(jnp.int32, (slots, rows), 0)
+        slot_id = jnp.where(slot_id >= cap, slot_id - cap, slot_id).astype(jnp.float32)
+        for j in range(seq_n):
+            offset = target_all[j] - s * rows
+            mine = (offset >= 0) & (offset < rows)
+            flag = jnp.where(mine, 1.0, 0.0)
+            rank = dot(flag.astype(jnp.bfloat16), before)
+            rank = jnp.where(mine, rank, -1.0)
+            filled = jnp.where(slot_id == rank[0:1, :], 1.0, 0.0).astype(jnp.bfloat16)
+            at = jnp.where(down == offset[0:1, :], 1.0, 0.0).astype(jnp.bfloat16)
+            marks_ref[j] = dot(filled, at, 1, 1).astype(jnp.bfloat16)
+
+    def send_rows():
+        started = ([], [])
+        for k, to in others():
+            cp = remote(vparcel.at[to], vgot.at[s], v_s.at[k], v_r.at[k], p, to)
+            cp.start()
+            started[0].append(cp)
+        for k, to in others():
+            cp = remote(parcel.at[to], got.at[s], par_s.at[k], par_r.at[k], p, to)
+            cp.start()
+            started[1].append(cp)
+        return started
+
+    left, right = packers()
+    vparcel[...] = (
+        (dot(left, value_ref[:, 0:vhalf]) + dot(right, value_ref[:, vhalf:]))
+        .astype(jnp.bfloat16).reshape(seq_n, slots, vhalf)
+    )
+    vgot[s] = vparcel[s]
+    parcel[...] = (
+        (dot(left, query_ref[:, 0:qhalf]) + dot(right, query_ref[:, qhalf:]))
+        .astype(jnp.bfloat16).reshape(seq_n, slots, qhalf)
+    )
+    got[s] = parcel[s]
+    pl.semaphore_wait(barrier, seq_n - 1 + dp_n - 1)
     for k, to in others():
         cp = remote(target_ref, target_all.at[s], tgt_s.at[k], tgt_r.at[k], p, to)
         cp.start()
         tgts.append(cp)
-    target_all[s] = target_ref[...]
-
-    left = left_ref[...]
-    right = right_ref[...]
-
-    def send_queries():
-        parcel[...] = (
-            (dot(left, query_ref[:, 0:qhalf]) + dot(right, query_ref[:, qhalf:]))
-            .astype(jnp.bfloat16).reshape(seq_n, slots, qhalf)
-        )
-        started = []
-        for k, to in others():
-            cp = remote(parcel.at[to], got.at[s], par_s.at[k], par_r.at[k], p, to)
-            cp.start()
-            started.append(cp)
-        got[s] = parcel[s]
-        kparcel[:, :, vhalf:] = (
-            (dot(left, value_ref[:, 0:vhalf]) + dot(right, value_ref[:, vhalf:]))
-            .astype(jnp.bfloat16).reshape(seq_n, slots, vhalf)
-        )
-        return started
-
-    par = []
+
     if inside:
         cores, ys, xs = [], [], []
 
@@ -190,19 +245,23 @@
             levels, a, lambda t: (p, t * 2 + b), wz_s, wz_r,
             lambda shard: wall.at[p, shard * 2 + b], held_w,
         )
-        par = send_queries()
+        vs, par = send_rows()
         for cp, index, sh in xs:
             cp.wait_recv()
             to_y(sh, 2 * index + 1)
         for cp, m, slot, sh in list(ys):
             cp.wait_recv()
             to_core(lax.rem(yb - m + nb, nb), sh, m * seq_n + slot)
+        places()
+        labels()
         for cp in cores:
             cp.wait_recv()
         sends += zc + [c[0] for c in xs] + [c[0] for c in ys] + cores
         weights = wall[...].reshape(hidden_ref.shape[1], -1)
     else:
-        par = send_queries()
+        vs, par = send_rows()
+        places()
+        labels()
         weights = w_ref[...]
 
     projected = dot(hidden_ref[...], weights)
@@ -215,7 +274,7 @@
         ],
         axis=1,
     ).astype(jnp.bfloat16)
-    kparcel[:, :, 0:vhalf] = (
+    kparcel[...] = (
         (dot(left, keys[:, 0:vhalf]) + dot(right, keys[:, vhalf:]))
         .astype(jnp.bfloat16).reshape(seq_n, slots, vhalf)
     )
@@ -226,77 +285,71 @@
         ks.append(cp)
     kgot[s] = kparcel[s]
 
-    for cp in tgts:
-        cp.wait_recv()
-    square = (rows, rows)
-    down = lax.broadcasted_iota(jnp.int32, square, 0)
-    across = lax.broadcasted_iota(jnp.int32, square, 1)
-    before = jnp.where(down < across, 1.0, 0.0).astype(jnp.bfloat16)
-    slot_id = lax.broadcasted_iota(jnp.int32, (slots, rows), 0)
-    slot_id = jnp.where(slot_id >= cap, slot_id - cap, slot_id).astype(jnp.float32)
-    for j in range(seq_n):
-        offset = target_all[j] - s * rows
-        mine = (offset >= 0) & (offset < rows)
-        flag = jnp.where(mine, 1.0, 0.0)
-        rank = dot(flag.astype(jnp.bfloat16), before)
-        rank = jnp.where(mine, rank, -1.0)
-        filled = jnp.where(slot_id == rank[0:1, :], 1.0, 0.0).astype(jnp.bfloat16)
-        at = jnp.where(down == offset[0:1, :], 1.0, 0.0).astype(jnp.bfloat16)
-        marks_ref[j] = dot(filled, at, 1, 1).astype(jnp.bfloat16)
     marks = marks_ref[...].reshape(seq_n * slots, rows)
     place = lax.rem(lax.broadcasted_iota(jnp.int32, marks.shape, 0), slots)
     first = jnp.where(place < cap, marks, jnp.zeros_like(marks))
     second = jnp.where(place < cap, jnp.zeros_like(marks), marks)
 
+    held_rows = seq_n * slots
+
+    def settle(ref, first_head):
+        block = ref[...].reshape(held_rows, vhalf)
+        for half, mark in ((0, first), (1, second)):
+            settled = dot(mark, block, 0, 0).astype(jnp.bfloat16)
+            for h in range(kvn // 2):
+                kv_win[first_head + half * (kvn // 2) + h, SPAN * rows:, :] = settled[
+                    :, h * HEAD_DIM:(h + 1) * HEAD_DIM
+                ]
+
+    def shift(by, head):
+        return remote(
+            kv_win.at[head, SPAN * rows:(SPAN + 1) * rows, :],
+            kv_win.at[head, (SPAN - by) * rows:(SPAN - by + 1) * rows, :],
+            sh_s.at[by - 1, head], sh_r.at[by - 1, head], p, lax.rem(s + by, seq_n),
+        )
+
+    def shift_all(first_head):
+        for head in range(kvn):
+            for by in range(1, SPAN + 1):
+                @pl.when(s + by < seq_n)
+                def _(by=by, head=head):
+                    shift(by, first_head + head).start()
+
+    for cp in vs:
+        cp.wait_recv()
+    settle(vgot, kvn)
+    shift_all(kvn)
+    for by in range(1, SPAN + 1):
+        @pl.when(s < by)
+        def _(by=by):
+            kv_win[:, (SPAN - by) * rows:(SPAN - by + 1) * rows, :] = jnp.zeros(
+                (2 * kvn, rows, HEAD_DIM), jnp.bfloat16
+            )
+
+        @pl.when(s + by >= seq_n)
+        def _(by=by):
+            back[by - 1] = jnp.zeros(back.shape[1:], jnp.bfloat16)
+    for cp in ks:
+        cp.wait_recv()
+    settle(kgot, 0)
+    shift_all(0)
     for cp in par:
         cp.wait_recv()
     for half, mark in ((0, first), (1, second)):
         base = half * (heads // 2)
-        settled = dot(mark, got[...].reshape(seq_n * slots, qhalf), 0, 0).astype(jnp.bfloat16)
+        settled = dot(mark, got[...].reshape(held_rows, qhalf), 0, 0).astype(jnp.bfloat16)
         for h in range(heads // 2):
             head = base + h
             q_seq[head // group, (head % group) * rows:(head % group + 1) * rows, :] = settled[
                 :, h * HEAD_DIM:(h + 1) * HEAD_DIM
             ]
-    for cp in ks:
-        cp.wait_recv()
-    for half, mark in ((0, first), (1, second)):
-        settled = dot(mark, kgot[...].reshape(seq_n * slots, 2 * vhalf), 0, 0).astype(jnp.bfloat16)
-        for h in range(kvn):
-            head = (h // (kvn // 2)) * kvn + half * (kvn // 2) + h % (kvn // 2)
-            kv_win[head, SPAN * rows:, :] = settled[:, h * HEAD_DIM:(h + 1) * HEAD_DIM]
-
-    def shift(by):
-        return remote(
-            kv_win.at[:, SPAN * rows:(SPAN + 1) * rows, :],
-            kv_win.at[:, (SPAN - by) * rows:(SPAN - by + 1) * rows, :],
-            sh_s.at[by], sh_r.at[by], p, lax.rem(s + by, seq_n),
-        )
-
-    for by in range(1, SPAN + 1):
-        @pl.when(s + by < seq_n)
-        def _(by=by):
-            shift(by).start()
-
-        @pl.when(s < by)
-        def _(by=by):
-            kv_win[:, (SPAN - by) * rows:(SPAN - by + 1) * rows, :] = jnp.zeros(
-                (2 * kvn, rows, HEAD_DIM), jnp.bfloat16
-            )
-
-        @pl.when(s + by >= seq_n)
-        def _(by=by):
-            back[by - 1] = jnp.zeros(back.shape[1:], jnp.bfloat16)
     cols = []
     for k, to in others():
         cp = remote(cols_ref.at[to], cols_all.at[s], col_s.at[k], col_r.at[k], p, to)
         cp.start()
         cols.append(cp)
     cols_all[s] = cols_ref[s]
-    for by in range(1, SPAN + 1):
-        @pl.when(s >= by)
-        def _(by=by):
-            shift(by).wait_recv()
+    starting = jnp.concatenate([lower] * group, axis=1)
 
     width = (SPAN + 1) * rows
     lanes = group * rows
@@ -310,11 +363,17 @@
         )
 
     def attend(g, carry):
+        for by in range(1, SPAN + 1):
+            @pl.when(s >= by)
+            def _(by=by):
+                shift(by, g).wait_recv()
+                shift(by, kvn + g).wait_recv()
+
         queries = q_seq[g]
         score = dot(kv_win[g], queries, 1, 1) * scaling
         spot = lax.broadcasted_iota(jnp.int32, (width, lanes), 0)
         last = lax.rem(lax.broadcasted_iota(jnp.int32, (1, lanes), 1), rows) + (width - rows)
-        allowed = (spot >= start_ref[...]) & (spot <= last)
+        allowed = (spot >= starting) & (spot <= last)
         held = jnp.where(allowed, score, negative)
         top = jnp.max(held, axis=0, keepdims=True)
         raised = jnp.exp(held - top)
@@ -354,16 +413,6 @@
 
     lax.fori_loop(0, kvn, attend, 0)
 
-    for cp in cols:
-        cp.wait_recv()
-    count = seq_n * rows
-    total = jnp.zeros((count, cols_ref.shape[2]), jnp.float32)
-    spot = lax.broadcasted_iota(jnp.int32, (count, rows), 0)
-    for j in range(seq_n):
-        hit = jnp.where(spot == target_all[j, 0:1, :], 1.0, 0.0).astype(jnp.bfloat16)
-        total += dot(hit, cols_all[j])
-    sorted_cols[...] = total.astype(jnp.bfloat16).reshape(sorted_cols.shape)
-
     for by in range(1, SPAN + 1):
         @pl.when(s + by < seq_n)
         def _(by=by):
@@ -391,6 +440,15 @@
     zk = spread(
         levels, a, lambda t: (p, t * 2 + b), z_s, z_r, lambda shard: kg.at[shard * 2 + b], held_kg
     )
+    for cp in cols:
+        cp.wait_recv()
+    count = seq_n * rows
+    total = jnp.zeros((count, cols_ref.shape[2]), jnp.float32)
+    spot = lax.broadcasted_iota(jnp.int32, (count, rows), 0)
+    for j in range(seq_n):
+        hit = jnp.where(spot == target_all[j, 0:1, :], 1.0, 0.0).astype(jnp.bfloat16)
+        total += dot(hit, cols_all[j])
+    sorted_cols[...] = total.astype(jnp.bfloat16).reshape(sorted_cols.shape)
     result = None
     for sh in terms:
         term = dot(sorted_cols[sh], kg[sh], 0, 0)
@@ -413,12 +471,13 @@
         ds[m - 1].wait_recv()
         final += arrived[m].astype(jnp.float32)
     out_ref[...] = final
-    for cp in sends + tgts + par + ks + cols + zk + [c[0] for c in pairs] + ds:
+    for cp in sends + tgts + vs + par + ks + cols + zk + [c[0] for c in pairs] + ds:
         cp.wait_send()
     for by in range(1, SPAN + 1):
         @pl.when(s + by < seq_n)
         def _(by=by):
-            shift(by).wait_send()
+            for head in range(2 * kvn):
+                shift(by, head).wait_send()
 
         @pl.when(s >= by)
         def _(by=by):
@@ -445,18 +504,10 @@
     dma = pltpu.SemaphoreType.DMA
     bf16 = jnp.bfloat16
 
-    destination = row_target // rows
     order = jnp.arange(rows, dtype=jnp.int32)
-    earlier = (destination[None, :] == destination[:, None]) & (order[None, :] < order[:, None])
-    rank = jnp.sum(earlier.astype(jnp.int32), axis=1)
-    slot = destination * slots + rank
-    every = jnp.arange(seq_n * slots, dtype=jnp.int32)[:, None]
-    left = (every == slot[None, :]).astype(bf16)
-    right = (every == slot[None, :] + capacity).astype(bf16)
     cos_row, sin_row = angles(row_target)
     columns = hidden.reshape(rows, dp_n, seq_n, depth).transpose(2, 0, 1, 3)
     columns = columns.reshape(seq_n, rows, dp_n * depth)
-    target_tile = jnp.broadcast_to(row_target[None, :], (8, rows))
 
     positions = s * rows + order
     ending = jnp.cumsum(dialogue_lengths[0])
@@ -464,12 +515,7 @@
         jnp.where(ending[None, :] <= positions[:, None], dialogue_lengths[0][None, :], 0), axis=1
     )
     base = (s - SPAN) * rows
-    reach = (positions - starts + 1)[:, None]
-    picks = (starts[:, None] - base + teacher_pick % reach).reshape(rows, kvn, group, top)
-    picks = picks.transpose(1, 3, 2, 0).reshape(kvn, top, group * rows)
-    probs = teacher_prob.reshape(rows, kvn, group, top).transpose(1, 3, 2, 0)
-    probs = probs.reshape(kvn, top, group * rows)
-    lower = jnp.tile(starts - base, group)[None, :]
+    lower = (starts - base)[None, :]
     cos_pos, sin_pos = angles(positions)
 
     inside = depth % 16 == 0
@@ -481,8 +527,8 @@
     wall = (dp_n, seq_n, depth, kv_width) if inside else (8, 128)
     link = bf16 if inside else jnp.float32
     semaphores = (
-        [(na,)] * 4 + [(nb, seq_n)] * 2 + [(nb * seq_n,)] * 2 + [(seq_n,)] * 8 + [(SPAN + 1,)] * 2
-        + [(SPAN, kvn)] * 2 + [(na,)] * 4 + [(dp_n,)] * 2
+        [(na,)] * 4 + [(nb, seq_n)] * 2 + [(nb * seq_n,)] * 2 + [(seq_n,)] * 10
+        + [(SPAN, 2 * kvn)] * 2 + [(SPAN, kvn)] * 2 + [(na,)] * 4 + [(dp_n,)] * 2
     )
     attn_out, loss, weight_grad = pl.pallas_call(
         functools.partial(
@@ -493,14 +539,19 @@
             jax.ShapeDtypeStruct((1, rows), jnp.float32),
             jax.ShapeDtypeStruct((depth, kv_width), jnp.float32),
         ),
-        in_specs=[vmem] * 15,
+        in_specs=[vmem] * 13,
         out_specs=(vmem,) * 3,
         scratch_shapes=[
             pltpu.VMEM(wall, bf16),
             pltpu.VMEM((seq_n, slots, qhalf), bf16),
             pltpu.VMEM((seq_n, slots, qhalf), bf16),
-            pltpu.VMEM((seq_n, slots, kv_width), bf16),
-            pltpu.VMEM((seq_n, slots, kv_width), bf16),
+            pltpu.VMEM((seq_n, slots, kv_width // 2), bf16),
+            pltpu.VMEM((seq_n, slots, kv_width // 2), bf16),
+            pltpu.VMEM((seq_n, slots, kv_width // 2), bf16),
+            pltpu.VMEM((seq_n, slots, kv_width // 2), bf16),
+            pltpu.VMEM((8, rows), jnp.int32),
+            pltpu.VMEM((kvn, top, group * rows), jnp.int32),
+            pltpu.VMEM((kvn, top, group * rows), jnp.float32),
             pltpu.VMEM((seq_n, slots, rows), bf16),
             pltpu.VMEM((kvn, group * rows, HEAD_DIM), bf16),
             pltpu.VMEM((2 * kvn, (SPAN + 1) * rows, HEAD_DIM), bf16),
@@ -518,8 +569,8 @@
             collective_id=0, has_side_effects=True, vmem_limit_bytes=VMEM_BYTES
         ),
     )(
-        weight_in, hidden, queries, values, left, right, cos_row, sin_row, columns, target_tile,
-        picks, probs, lower, cos_pos, sin_pos,
+        weight_in, hidden, queries, values, row_target[None, :], cos_row, sin_row, columns,
+        teacher_pick, teacher_prob, lower, cos_pos, sin_pos,
     )
     return attn_out, loss[0], weight_grad
 

time: 99.3 us -> 90.3 us (0.909); the launches traced: 97.8 us -> 90 us
  Pallas kernels: 88.5 us -> 83.2 us
  other arithmetic: 2.78 us -> 1.14 us
    pallas_call x1, Pallas kernels: 88.5 us -> 83.2 us  [local(): pl.pallas_call(functools.partial(whole_kernel, seq_n, dp_n, inside, (rows...]
where the time goes in v3:
time: 90.3 us; the launch traced here: 90 us
  Pallas kernels  83.2 us (92%)
  local copies, waits for them, and re-layouts  4.81 us (5%)
  other arithmetic  1.14 us (1%)
    pallas_call x1, Pallas kernels, local(): pl.pallas_call(functools.partial(whole_kernel, seq_n, dp_n, inside, (rows...  83.2 us
    unnamed x20, local copies, waits for them, and re-layouts  4.47 us

profile of v3, /device:TPU:0, one launch (start us, length us, event | category | flops | bytes accessed | tf_op | source)
XLA Modules:
  0.0 90.0 jit_solution(5369286150587980690)
XLA Ops:
  0.6 0.6 copy-done.6
  1.3 0.0 copy-start.7
  1.3 0.6 copy-done.7
  2.0 0.1 copy.19
  2.1 0.1 reduce
  2.2 0.1 select_reduce_fusion
  2.3 0.5 fusion.1
  2.9 0.1 pad_maximum_fusion.3.sinpos_ref
  3.0 0.1 pad_maximum_fusion.2.cospos_ref
  3.0 0.1 pad_maximum_fusion.cos_ref
  3.1 0.1 pad_maximum_fusion.1.sin_ref
  3.2 0.1 copy-done
  3.4 0.3 copy.17
  3.7 0.0 copy-start.1
  3.7 0.0 copy-start.2
  3.7 0.0 copy-start.3
  3.7 0.2 copy.20.cols_ref
  4.0 0.8 copy-done.1
  4.7 0.0 copy-done.2
  4.7 0.0 copy-done.5
  4.8 83.2 %shard_map.103 = (bf16[128,2048]{1,0:T(8,128)(2,1)S(1)}, f32[1,128]{1,0:T(1,128)S(1)}, f32[64,512]{1,0:T(8,128)S(1)}) custom-call(bf16[64,512]{1,0:T(8,128)(2,1)S(1)} %copy-done.3, bf16[128,2048]{1,0:T(8,128)(2,1)S(1)} %copy-done, bf16[128,2048]{1,0:T(8,128)(2,1)S(1)} %copy-done.1, bf16[128,512]{1,0:T(8,128)(2,1)S(1)} %copy-done.2, s32[1,128]{1,0:T(1,128)S(1)} %bitcast.10, ...), custom_call_target="tpu_custom_call" | custom-call | tf_op jit(solution)/shard_map/pallas_call | solution.py:533
  88.0 0.8 copy.24
  88.8 0.5 copy.25
  89.3 0.7 copy.26
  (12 shorter events, 0.1 us)
Async XLA Ops:
  0.6 0.7 copy-start.6
  1.3 0.7 copy-start.7
  2.3 1.0 %copy-start = (bf16[128,2048]{1,0:T(8,128)(2,1)S(1)}, bf16[128,2048]{1,0:T(8,128)(2,1)}, u32[]{:S(2)}) copy-start(bf16[128,2048]{1,0:T(8,128)(2,1)} %hidden_ref.1) | copy-start | bytes 1572868
  3.7 1.0 %copy-start.1 = (bf16[128,2048]{1,0:T(8,128)(2,1)S(1)}, bf16[128,2048]{1,0:T(8,128)(2,1)}, u32[]{:S(2)}) copy-start(bf16[128,2048]{1,0:T(8,128)(2,1)} %query_ref.1) | copy-start | bytes 1572868
  3.7 1.1 %copy-start.2 = (bf16[128,512]{1,0:T(8,128)(2,1)S(1)}, bf16[128,512]{1,0:T(8,128)(2,1)}, u32[]{:S(2)}) copy-start(bf16[128,512]{1,0:T(8,128)(2,1)} %value_ref.1) | copy-start | bytes 393220
  3.7 1.0 %copy-start.3 = (bf16[64,512]{1,0:T(8,128)(2,1)S(1)}, bf16[64,512]{1,0:T(8,128)(2,1)}, u32[]{:S(2)}) copy-start(bf16[64,512]{1,0:T(8,128)(2,1)} %w_ref.1) | copy-start | bytes 196612
  3.7 1.0 %copy-start.4 = (s32[128,128]{1,0:T(8,128)S(1)}, s32[128,128]{1,0:T(8,128)}, u32[]{:S(2)}) copy-start(s32[128,128]{1,0:T(8,128)} %drawn_ref.1) | copy-start | bytes 196612
  3.7 1.0 %copy-start.5 = (f32[128,128]{1,0:T(8,128)S(1)}, f32[128,128]{1,0:T(8,128)}, u32[]{:S(2)}) copy-start(f32[128,128]{1,0:T(8,128)} %given_ref.1) | copy-start | bytes 196612
